TPU v7x, 32 devices: a whole 2x2x4 slice. The times are simulated.
32 devices in a mesh: dp: 16 (over z, x, core), tensor: 2 (over y).
Axes of the slice: x: 2, y: 2, z: 4, core: 2. Of those that a mesh axis runs over, the one named last changes fastest.
Arguments:
- hidden_input_state: bfloat16 [6144, 4608], P('dp', 'tensor'), may hold values from -80 to 80
- norm_gain: float32 [4608], replicated, may hold values from 0.5 to 1.5
- head_weight: bfloat16 [4608, 2048], P(None, 'tensor'), may hold values from -2 to 2
- target_ids: int32 [6144], P('dp'), may hold values from 0 to 2047
Outputs:
- hidden_state_gradient: float32 [6144, 4608], P('dp', 'tensor')
- grad_head: float32 [4608, 2048], P('dp', 'tensor')
- norm_gain_gradient: float32 [4608], P('tensor')
All inputs are finite; a program needn't handle non-finite values.
Results may differ from a plain program's by a relative error of at most 0.0039.
Values may be sent and summed in bfloat16 or wider, within the bound.
A program may use at most 192 MiB of HBM per device.

v0:
```python
import jax
import jax.numpy as jnp
from jax import lax
from jax.sharding import PartitionSpec as P

epsilon = 1e-06


def shards(hidden_input_state, norm_gain, head_weight, target_ids):
    local_cols = hidden_input_state.shape[1]
    vocab_rows = head_weight.shape[1]
    width = head_weight.shape[0]
    gathered = lax.all_gather(hidden_input_state, "tensor", axis=1, tiled=True)
    values = gathered.astype(jnp.float32)
    scaled_rows = lax.rsqrt(jnp.mean(values * values, axis=1, keepdims=True) + epsilon)
    normed = (values * scaled_rows * norm_gain[None, :]).astype(jnp.bfloat16)
    logits = jnp.dot(normed, head_weight, preferred_element_type=jnp.float32)
    local_top = jnp.max(logits, axis=1)
    local_total = jnp.sum(jnp.exp(logits - local_top[:, None]), axis=1)
    row_top = lax.pmax(local_top, "tensor")
    row_total = lax.psum(local_total * jnp.exp(local_top - row_top), "tensor")
    log_total = row_top + jnp.log(row_total)
    offset = lax.axis_index("tensor") * vocab_rows
    column_ids = offset + lax.broadcasted_iota(jnp.int32, (1, vocab_rows), 1)
    onehot = (column_ids == target_ids[:, None]).astype(jnp.float32)
    dlogits = (jnp.exp(logits - log_total[:, None]) - onehot).astype(jnp.bfloat16)
    start_col = lax.axis_index("tensor") * local_cols
    normalized_slice = hidden_input_state.astype(jnp.float32) * scaled_rows
    gain_slice = lax.dynamic_slice_in_dim(norm_gain, start_col, local_cols)
    grad_cols = lax.psum_scatter(
        lax.dot_general(
            head_weight, dlogits, (((1,), (1,)), ((), ())), preferred_element_type=jnp.float32
        ),
        "tensor",
        scatter_dimension=0,
        tiled=True,
    )
    normed_gradient = grad_cols.T
    partial_inner_sum = jnp.sum(normed_gradient * gain_slice[None, :] * normalized_slice, axis=1)
    row_inner_sum = lax.psum(partial_inner_sum, "tensor") / width
    weighted_rows = normed_gradient * gain_slice[None, :]
    hidden_state_gradient = scaled_rows * (
        weighted_rows - normalized_slice * row_inner_sum[:, None]
    )
    norm_gain_gradient = lax.psum(jnp.sum(normed_gradient * normalized_slice, axis=0), "dp")
    grad_head = lax.psum_scatter(
        lax.dot_general(
            normed, dlogits, (((0,), (0,)), ((), ())), preferred_element_type=jnp.float32
        ),
        "dp",
        scatter_dimension=0,
        tiled=True,
    )
    return (hidden_state_gradient, grad_head, norm_gain_gradient)


def solution(mesh):
    return jax.shard_map(
        shards,
        mesh=mesh,
        in_specs=(P("dp", "tensor"), P(), P(None, "tensor"), P("dp")),
        out_specs=(P("dp", "tensor"), P("dp", "tensor"), P("tensor")),
        check_vma=False,
    )
```

profile of v0, /device:TPU:0, one launch (start us, length us, event | category | flops | bytes accessed | tf_op | source)
XLA Modules:
  0.0 389.3 jit_solution(7400442858176294331)
XLA Ops:
  7.2 0.0 all-gather.2.cloned.1.call-start
  7.2 0.7 all-gather.2.cloned.1.call-update
  7.9 0.0 reduce-scatter.3.cloned.1.call-start
  8.0 53.7 %all-gather.2.cloned.1.call-done = bf16[384,4608]{1,0:T(8,128)(2,1)} async-done(((bf16[384,2304]{1,0:T(8,128)(2,1)}), bf16[384,4608]{1,0:T(8,128)(2,1)}) %all-gather.2.cloned.1.call-update) | async-done | bytes 3538960 | tf_op jit(solution)/shard_map/all_gather | solution.py:13
  61.6 0.0 copy-start.1
  61.6 2.9 fusion
  64.6 0.1 copy-done.1
  64.7 7.8 %fusion.8 = (f32[384]{0:T(512)S(1)}, f32[384,1024]{1,0:T(8,128)}) fusion(bf16[4608,1024]{1,0:T(8,128)(2,1)} %param.6, bf16[384,4608]{1,0:T(8,128)(2,1)S(1)} %copy-done.1, f32[4608]{0:T(1024)} %param.5, f32[384]{0:T(512)S(1)} %add_rsqrt_fusion), kind=kOutput, calls=%fused_computation.21 | convolution fusion | flops 3631349248 | bytes 14570496 | tf_op jit(solution)/shard_map/dot_general | solution.py:17
  72.5 4.9 %pmax.7 = f32[384]{0:T(512)S(1)} all-reduce(f32[384]{0:T(512)S(1)} %get-tuple-element.5), channel_id=1, replica_groups=mesh['dp'=16,'tensor'=2] {'tensor'}, use_global_device_ids=true, to_apply=%region_2.0 | all-reduce | flops 384 | bytes 3072 | tf_op jit(solution)/shard_map/pmax | solution.py:20
  77.4 1.8 exponential_reduce_fusion
  79.2 0.6 exponential_multiply_fusion
  79.8 5.6 %psum.21 = f32[384]{0:T(512)} all-reduce(f32[384]{0:T(512)} %exponential_multiply_fusion), channel_id=1, replica_groups=mesh['dp'=16,'tensor'=2] {'tensor'}, use_global_device_ids=true, to_apply=%region_4.0 | all-reduce | flops 384 | bytes 3072 | tf_op jit(solution)/shard_map/psum | solution.py:21
  85.4 0.7 log_add_fusion
  86.1 11.0 %convolution_bitcast_fusion = f32[4608,384]{0,1:T(8,128)} fusion(bf16[4608,1024]{1,0:T(8,128)(2,1)} %param.6, f32[384,1024]{1,0:T(8,128)} %get-tuple-element.6, s32[1024]{0:T(1024)S(1)} %iota_add_fusion, f32[384]{0:T(512)S(1)} %log_add_fusion, s32[384]{0:T(512)} %param.7), kind=kOutput, calls=%fused_computation.2 | convolution fusion | flops 3625844736 | bytes 18095104 | tf_op jit(solution)/shard_map/dot_general | solution.py:31
  97.1 0.0 copy-start.3
  97.1 0.0 reduce-scatter.3.cloned.1.call-update
  97.1 0.0 reduce-scatter.5.cloned.1.call-start
  97.2 0.6 copy-done.3
  97.8 11.4 %fusion.4 = f32[4608,1024]{1,0:T(8,128)} fusion(bf16[384,4608]{1,0:T(8,128)(2,1)S(1)} %copy-done.1, f32[4608]{0:T(1024)} %param.5, f32[384]{0:T(512)S(1)} %add_rsqrt_fusion, f32[384,1024]{1,0:T(8,128)} %get-tuple-element.6, s32[1024]{0:T(1024)S(1)} %iota_add_fusion, f32[384]{0:T(512)S(1)} %log_add_fusion, s32[384]{0:T(512)S(1)} %copy-done.3), kind=kOutput, calls=%fused_computation.14 | convolution fusion | flops 3632922624 | bytes 24013312 | tf_op jit(solution)/shard_map/dot_general | solution.py:47
  109.3 0.0 copy-start.2
  109.3 0.0 copy-start
  109.3 0.0 reduce-scatter.5.cloned.1.call-update
  109.3 0.7 copy-done.2
  110.0 0.1 dynamic_slice.3
  110.1 72.9 %reduce-scatter.3.cloned.1.call-done = f32[2304,384]{0,1:T(8,128)} async-done(((f32[4608,384]{0,1:T(8,128)}), f32[2304,384]{0,1:T(8,128)}) %reduce-scatter.3.cloned.1.call-update) | async-done | bytes 3538960 | tf_op jit(solution)/shard_map/reduce_scatter | solution.py:30
  182.9 0.0 copy-done
  182.9 3.0 fusion.3
  185.9 4.9 %psum.22 = f32[384]{0:T(512)S(1)} all-reduce(f32[384]{0:T(512)S(1)} %get-tuple-element.4), channel_id=1, replica_groups=mesh['dp'=16,'tensor'=2] {'tensor'}, use_global_device_ids=true, to_apply=%region_7.0 | all-reduce | flops 384 | bytes 3072 | tf_op jit(solution)/shard_map/psum | solution.py:40
  190.9 61.7 %psum.23 = f32[2304]{0:T(1024)} all-reduce(f32[2304]{0:T(1024)S(1)} %get-tuple-element.3), channel_id=1, replica_groups=mesh['dp'=16,'tensor'=2] {'dp'}, use_global_device_ids=true, to_apply=%region_10.0 | all-reduce | flops 2304 | bytes 18432 | tf_op jit(solution)/shard_map/psum | solution.py:45
  252.6 4.7 %subtract_multiply_fusion = f32[384,2304]{1,0:T(8,128)} fusion(bf16[384,2304]{1,0:T(8,128)(2,1)S(1)} %copy-done, f32[2304,384]{0,1:T(8,128)} %reduce-scatter.3.cloned.1.call-done, f32[384]{0:T(512)S(1)} %broadcast_multiply_fusion, f32[2304]{0:T(1024)S(1)} %dynamic_slice.3, f32[384]{0:T(512)S(1)} %add_rsqrt_fusion), kind=kLoop, calls=%fused_computation.9 | loop fusion | flops 5308416 | bytes 8859648 | tf_op jit(solution)/shard_map/mul | solution.py:42
  257.3 125.5 %reduce-scatter.5.cloned.1.call-done = f32[288,1024]{1,0:T(8,128)} async-done(((f32[4608,1024]{1,0:T(8,128)}), f32[288,1024]{1,0:T(8,128)}) %reduce-scatter.5.cloned.1.call-update) | async-done | bytes 1179664 | tf_op jit(solution)/shard_map/reduce_scatter | solution.py:46
  (3 shorter events, 0.0 us)
Async XLA Ops:
  7.2 54.5 %all-gather.2.cloned.1.call-start = ((), (), s32[]{:S(2)}) async-start(), calls=%async_computation.2 | async-start | bytes 5308416 | tf_op jit(solution)/shard_map/all_gather | solution.py:13
  7.9 175.0 %reduce-scatter.3.cloned.1.call-start = ((), (), s32[]{:S(2)}) async-start(), calls=%async_computation.3 | async-start | bytes 10616832 | tf_op jit(solution)/shard_map/reduce_scatter | solution.py:30
  61.6 3.1 copy-start.1
  97.1 0.7 copy-start.3
  97.1 285.6 %reduce-scatter.5.cloned.1.call-start = ((), (), s32[]{:S(2)}) async-start(), calls=%async_computation.4 | async-start | bytes 20054016 | tf_op jit(solution)/shard_map/reduce_scatter | solution.py:46
  109.3 0.7 copy-start.2
  109.3 73.7 %copy-start = (bf16[384,2304]{1,0:T(8,128)(2,1)S(1)}, bf16[384,2304]{1,0:T(8,128)(2,1)}, u32[]{:S(2)}) copy-start(bf16[384,2304]{1,0:T(8,128)(2,1)} %param.4) | copy-start | bytes 5308420
Sparse Core Ops, SparseCore 0:
  9.5 52.0 all-gather.1
  97.3 85.5 reduce-scatter.2
  188.2 194.5 reduce-scatter.4
where the time goes:
time: 390 us; the launch traced here: 389 us
  waiting for transfers between devices  253 us (65%)
  blocking collectives  77.2 us (20%)
  matrix products  30.3 us (8%)
  between operations  13.8 us (4%)
  other arithmetic  13.7 us (4%)
    reduce_scatter x1, waiting for transfers between devices, shards(): lax.psum_scatter(lax.dot_general(normed, dlogits, (((0,), (0,)), ((), ())...  126 us
    reduce_scatter x1, waiting for transfers between devices, shards(): lax.psum_scatter(lax.dot_general(head_weight, dlogits, (((1,), (1,)), (()...  72.9 us
    psum x1, blocking collectives, shards(): lax.psum(jnp.sum(normed_gradient * normalized_slice, axis=0), 'dp')  61.7 us
    all_gather x1, waiting for transfers between devices, shards(): gathered = lax.all_gather(hidden_input_state, 'tensor', axis=1, tiled=True)  53.7 us
    dot_general x1, matrix products, shards(): lax.dot_general(normed, dlogits, (((0,), (0,)), ((), ())), preferred_elem...  11.4 us
    dot_general x1, matrix products, shards(): lax.dot_general(head_weight, dlogits, (((1,), (1,)), ((), ())), preferred...  11 us
  transfers between devices with their start and end apart: 3, of which 3 were waited for; matrix products, arithmetic and copies ran while one was open for 5% of the time, Pallas kernels for 0%

commit v1 on v0

v1 whole, which is shorter than its diff:
```python
import jax
import jax.numpy as jnp
from jax import lax
from jax.sharding import PartitionSpec as P

epsilon = 1e-06
bf16 = jnp.bfloat16
f32 = jnp.float32


def make(mesh):
    nt = mesh.shape["tensor"]
    ndp = mesh.shape["dp"]
    nc = 2
    nb = 2
    na = ndp // (nc * nb)

    def shift_tensor(x, k):
        return lax.ppermute(x, "tensor", [(i, (i + k) % nt) for i in range(nt)])

    def dp_shift(x, da, db, dc):
        pairs = []
        for a in range(na):
            for b in range(nb):
                for c in range(nc):
                    src = (a * nb + b) * nc + c
                    dst = (((a + da) % na) * nb + (b + db) % nb) * nc + (c + dc) % nc
                    pairs.append((src, dst))
        return lax.ppermute(x, "dp", pairs)

    def shards(h, gain, head, targets):
        rows, cols = h.shape
        width, vocab = head.shape
        t = lax.axis_index("tensor")
        d = lax.axis_index("dp")
        a, b, c = d // (nb * nc), (d // nc) % nb, d % nc

        own_sq = jnp.sum(jnp.square(h.astype(f32)), axis=1)
        sq = own_sq
        for k in range(1, nt):
            sq = sq + shift_tensor(own_sq, k)
        nchunk = 3 if rows % 3 == 0 else 1
        step = rows // nchunk
        got = [[] for _ in range(nt)]
        for i in range(nchunk):
            piece = h[i * step:(i + 1) * step]
            got[0].append(piece)
            for k in range(1, nt):
                got[k].append(shift_tensor(piece, k))
        scaled = lax.rsqrt(sq / width + epsilon)

        def w_block(k):
            return lax.dynamic_slice_in_dim(head, ((t + k) % nt) * cols, cols, axis=0)

        def gain_block(k):
            return lax.dynamic_slice_in_dim(gain, ((t + k) % nt) * cols, cols)

        logit_parts = []
        normed_parts = []
        for i in range(nchunk):
            s = scaled[i * step:(i + 1) * step, None]
            full = jnp.zeros((step, width), bf16)
            for k in range(nt):
                g = gain_block(-k)[None, :]
                n = (got[k][i].astype(f32) * s * g).astype(bf16)
                full = lax.dynamic_update_slice_in_dim(full, n, ((t - k) % nt) * cols, axis=1)
            normed_parts.append(full)
            logit_parts.append(jnp.dot(full, head, preferred_element_type=f32))
        normed = jnp.concatenate(normed_parts, axis=0)
        logits = jnp.concatenate(logit_parts, axis=0)

        top = jnp.max(logits, axis=1)
        total = jnp.sum(jnp.exp(logits - top[:, None]), axis=1)
        stats = jnp.stack([top, total])
        all_stats = [stats] + [shift_tensor(stats, k) for k in range(1, nt)]
        row_top = top
        for s in all_stats[1:]:
            row_top = jnp.maximum(row_top, s[0])
        row_total = sum(s[1] * jnp.exp(s[0] - row_top) for s in all_stats)
        log_total = row_top + jnp.log(row_total)
        ids = t * vocab + lax.broadcasted_iota(jnp.int32, (1, vocab), 1)
        onehot = (ids == targets[:, None]).astype(f32)
        exact = jnp.exp(logits - log_total[:, None]) - onehot
        dlogits = exact.astype(bf16)
        dot_own = jnp.sum(dlogits.astype(f32) * logits, axis=1)
        dot_all = dot_own
        for k in range(1, nt):
            dot_all = dot_all + shift_tensor(dot_own, k)
        row_dot = dot_all / width

        arrived = []
        for k in range(1, nt):
            part = lax.dot_general(dlogits, w_block(k), (((1,), (1,)), ((), ())),
                                   preferred_element_type=f32).astype(bf16)
            arrived.append(shift_tensor(part, k))

        block = width // na
        small = width // ndp
        order = list(range(na // 2, 0, -1)) + list(range(na // 2 + 1, na)) + [0]
        pieces = []
        for k in order:
            to = (a + k) % na
            cut = lax.dynamic_slice_in_dim(normed, to * block, block, axis=1)
            prod = lax.dot_general(cut, dlogits, (((0,), (0,)), ((), ())),
                                   preferred_element_type=f32)
            prod = prod.reshape(nb, nc, small, vocab)
            keep = lax.dynamic_index_in_dim(prod, c, axis=1, keepdims=False)
            away = lax.dynamic_index_in_dim(prod, 1 - c, axis=1, keepdims=False).astype(bf16)
            keep = keep + dp_shift(away, 0, 0, 1).astype(f32)
            mine = lax.dynamic_index_in_dim(keep, b, axis=0, keepdims=False)
            other = lax.dynamic_index_in_dim(keep, 1 - b, axis=0, keepdims=False).astype(bf16)
            mine = mine + dp_shift(other, 0, 1, 0).astype(f32)
            if k:
                mine = dp_shift(mine.astype(bf16), k, 0, 0).astype(f32)
            pieces.append(mine)

        grad = lax.dot_general(dlogits, w_block(0), (((1,), (1,)), ((), ())),
                               preferred_element_type=f32)
        for p in arrived:
            grad = grad + p.astype(f32)
        normalized = h.astype(f32) * scaled[:, None]
        hidden = scaled[:, None] * (grad * gain_block(0)[None, :] - normalized * row_dot[:, None])
        gain_grad = jnp.sum(grad * normalized, axis=0)
        gain_grad = gain_grad + dp_shift(gain_grad, 0, 0, 1)
        gain_grad = gain_grad + dp_shift(gain_grad, 0, 1, 0)
        gain_grad = gain_grad + sum(dp_shift(gain_grad, k, 0, 0) for k in range(1, na))
        grad_head = pieces[-1]
        for p in pieces[:-1]:
            grad_head = grad_head + p
        return hidden, grad_head, gain_grad

    return shards


def solution(mesh):
    return jax.shard_map(
        make(mesh),
        mesh=mesh,
        in_specs=(P("dp", "tensor"), P(), P(None, "tensor"), P("dp")),
        out_specs=(P("dp", "tensor"), P("dp", "tensor"), P("tensor")),
        check_vma=False,
    )
```

time: 390 us -> 182 us (0.47)
  waiting for transfers between devices: 253 us -> 122 us
  blocking collectives: 77.2 us -> 0 us
  starting transfers between devices: 0.12 us -> 28.6 us
  between operations: 13.8 us -> 0.98 us
  matrix products: 30.3 us -> 19.6 us
  other arithmetic: 13.7 us -> 9.44 us
    reduce_scatter x2 -> x0, waiting for transfers between devices: 198 us -> none  [the longest x1 126 us: shards(): lax.psum_scatter(lax.dot_general(normed, dlogits, (((0,), (0,)), ((), ())...]
    ppermute x0 -> x23, waiting for transfers between devices: none -> 122 us  [the longest x7 66.4 us: shift_tensor(): return lax.ppermute(x, 'tensor', [(i, (i + k) % nt) for i in range(nt)])]
    psum x3 -> x0, blocking collectives: 72.3 us -> none  [the longest x1 61.7 us: shards(): lax.psum(jnp.sum(normed_gradient * normalized_slice, axis=0), 'dp')]
    all_gather x1 -> x0, waiting for transfers between devices: 53.7 us -> none  [shards(): gathered = lax.all_gather(hidden_input_state, 'tensor', axis=1, tiled=True)]
    ppermute x0 -> x23, starting transfers between devices: none -> 28.6 us  [the longest x16 17.6 us: dp_shift(): return lax.ppermute(x, 'dp', pairs)]
    dot_general x3 -> x9, matrix products: 30.3 us -> 19.6 us  [the longest x1 6 us: shards(): lax.dot_general(dlogits, w_block(0), (((1,), (1,)), ((), ())), preferred_...]
    mul x2 -> x0, other arithmetic: 5.29 us -> none  [the longest x1 4.69 us: shards(): scaled_rows * (weighted_rows - normalized_slice * row_inner_sum[:, None])]
    pmax x1 -> x0, blocking collectives: 4.92 us -> none  [shards(): row_top = lax.pmax(local_top, 'tensor')]
  transfers between devices with their start and end apart: 3 -> 23, of which waited for: 3 -> 14; matrix products, arithmetic and copies ran while one was open for 5% -> 9% of each run, Pallas kernels for 0% -> 0%
where the time goes in v1:
time: 182 us
  waiting for transfers between devices  122 us (67%)
  starting transfers between devices  28.6 us (16%)
  matrix products  19.6 us (11%)
  other arithmetic  9.44 us (5%)
    ppermute x7, waiting for transfers between devices, shift_tensor(): return lax.ppermute(x, 'tensor', [(i, (i + k) % nt) for i in range(nt)])  66.4 us
    ppermute x16, waiting for transfers between devices, dp_shift(): return lax.ppermute(x, 'dp', pairs)  55.8 us
    ppermute x16, starting transfers between devices, dp_shift(): return lax.ppermute(x, 'dp', pairs)  17.6 us
    ppermute x7, starting transfers between devices, shift_tensor(): return lax.ppermute(x, 'tensor', [(i, (i + k) % nt) for i in range(nt)])  11 us
    dot_general x1, matrix products, shards(): lax.dot_general(dlogits, w_block(0), (((1,), (1,)), ((), ())), preferred_...  6 us
    dot_general x4, matrix products, shards(): lax.dot_general(cut, dlogits, (((0,), (0,)), ((), ())), preferred_element...  5.75 us
    dot_general x3, matrix products, shards(): logit_parts.append(jnp.dot(full, head, preferred_element_type=f32))  4.64 us
  transfers between devices with their start and end apart: 23, of which 14 were waited for; matrix products, arithmetic and copies ran while one was open for 9% of the time, Pallas kernels for 0%

profile of v1, /device:TPU:0, one launch (start us, length us, event | category | flops | bytes accessed | tf_op | source)
XLA Modules:
  0.0 182.3 jit_solution(3184487505057907214)
XLA Ops:
  0.6 2.0 %fusion.12 = f32[384]{0:T(512)S(1)} fusion(bf16[384,2304]{1,0:T(8,128)(2,1)} %param.4), kind=kLoop, calls=%fused_computation.12 | loop fusion | flops 2653824 | bytes 1771008 | tf_op jit(solution)/shard_map/reduce_sum | solution.py:38
  2.7 3.0 %collective-permute-start = (f32[384]{0:T(512)S(1)}, f32[384]{0:T(512)S(1)}, u32[]{:S(2)}, u32[]{:S(2)}) collective-permute-start(f32[384]{0:T(512)S(1)} %fusion.12), channel_id=1, source_target_pairs={{0,1},{1,0},{2,3},{3,2},{4,5},{5,4},{6,7},{7,6},{8,9},{9,8},{10,11... | collective-permute-start | bytes 4616 | tf_op jit(solution)/shard_map/ppermute | solution.py:19
  5.8 1.5 collective-permute-done
  7.6 2.1 %collective-permute-start.1 = (bf16[128,2304]{1,0:T(8,128)(2,1)S(1)}, bf16[128,2304]{1,0:T(8,128)(2,1)S(1)}, u32[]{:S(2)}, u32[]{:S(2)}) collective-permute-start(bf16[128,2304]{1,0:T(8,128)(2,1)S(1)} %get-tuple-element.9), channel_id=1, source_target_pairs={{0,1},{1,0},{2,3},{3,2},{4,5},{5,4},{6,7},{7,6},{8,9},{9,8},{10,11... | collective-permute-start | bytes 1769480 | tf_op jit(solution)/shard_map/ppermute | solution.py:19
  9.8 1.9 %collective-permute-start.2 = (bf16[128,2304]{1,0:T(8,128)(2,1)S(1)}, bf16[128,2304]{1,0:T(8,128)(2,1)S(1)}, u32[]{:S(2)}, u32[]{:S(2)}) collective-permute-start(bf16[128,2304]{1,0:T(8,128)(2,1)S(1)} %get-tuple-element.12), channel_id=1, source_target_pairs={{0,1},{1,0},{2,3},{3,2},{4,5},{5,4},{6,7},{7,6},{8,9},{9,8},{10,11... | collective-permute-start | bytes 1769480 | tf_op jit(solution)/shard_map/ppermute | solution.py:19
  12.3 11.6 %collective-permute-done.1 = bf16[128,2304]{1,0:T(8,128)(2,1)S(1)} collective-permute-done((bf16[128,2304]{1,0:T(8,128)(2,1)S(1)}, bf16[128,2304]{1,0:T(8,128)(2,1)S(1)}, u32[]{:S(2)}, u32[]{:S(2)}) %collective-permute-start.1) | collective-permute-done | bytes 589856 | tf_op jit(solution)/shard_map/ppermute | solution.py:19
  24.0 12.6 %collective-permute-done.3 = bf16[128,2304]{1,0:T(8,128)(2,1)S(1)} collective-permute-done((bf16[128,2304]{1,0:T(8,128)(2,1)S(1)}, bf16[128,2304]{1,0:T(8,128)(2,1)S(1)}, u32[]{:S(2)}, u32[]{:S(2)}) %collective-permute-start.3) | collective-permute-done | bytes 589856 | tf_op jit(solution)/shard_map/ppermute | solution.py:19
  36.6 10.6 %collective-permute-done.2 = bf16[128,2304]{1,0:T(8,128)(2,1)S(1)} collective-permute-done((bf16[128,2304]{1,0:T(8,128)(2,1)S(1)}, bf16[128,2304]{1,0:T(8,128)(2,1)S(1)}, u32[]{:S(2)}, u32[]{:S(2)}) %collective-permute-start.2) | collective-permute-done | bytes 589856 | tf_op jit(solution)/shard_map/ppermute | solution.py:19
  47.7 1.5 fusion.55
  49.2 1.5 fusion.54
  50.8 1.6 fusion.53
  52.9 1.8 collective-permute-start.4
  55.0 1.6 collective-permute-done.4
  57.3 3.3 %fusion.6 = bf16[384,2304]{1,0:T(8,128)(2,1)} fusion(bf16[384,1024]{1,0:T(8,128)(2,1)S(1)} %get-tuple-element.6, bf16[4608,1024]{1,0:T(8,128)(2,1)S(1)} %copy-done, s32[]{:T(128)S(6)} %select_n.134), kind=kOutput, calls=%fused_computation.8 | convolution fusion | flops 1812824064 | bytes 7274500 | tf_op jit(solution)/shard_map/dot_general | solution.py:93
  60.5 1.7 collective-permute-start.5
  69.8 28.5 %collective-permute-done.6 = f32[384]{0:T(512)S(1)} collective-permute-done((f32[384]{0:T(512)S(1)}, f32[384]{0:T(512)S(1)}, u32[]{:S(2)}, u32[]{:S(2)}) %collective-permute-start.6) | collective-permute-done | bytes 1568 | tf_op jit(solution)/shard_map/ppermute | solution.py:19
  98.9 1.5 collective-permute-start.16
  102.4 1.5 collective-permute-start.10
  105.2 9.9 %collective-permute-done.16 = bf16[288,1024]{1,0:T(8,128)(2,1)S(1)} collective-permute-done((bf16[288,1024]{1,0:T(8,128)(2,1)S(1)}, bf16[288,1024]{1,0:T(8,128)(2,1)S(1)}, u32[]{:S(2)}, u32[]{:S(2)}) %collective-permute-start.16) | collective-permute-done | bytes 589856 | tf_op jit(solution)/shard_map/ppermute | solution.py:29
  115.3 3.6 %collective-permute-start.17 = (bf16[288,1024]{1,0:T(8,128)(2,1)S(1)}, bf16[288,1024]{1,0:T(8,128)(2,1)S(1)}, u32[]{:S(2)}, u32[]{:S(2)}) collective-permute-start(bf16[288,1024]{1,0:T(8,128)(2,1)S(1)} %fusion.17), channel_id=1, source_target_pairs={{0,24},{2,26},{4,28},{6,30},{8,0},{10,2},{12,4},{14,6},{16,8},{18,... | collective-permute-start | bytes 1769480 | tf_op jit(solution)/shard_map/ppermute | solution.py:29
  118.9 8.9 %collective-permute-done.13 = bf16[288,1024]{1,0:T(8,128)(2,1)S(1)} collective-permute-done((bf16[288,1024]{1,0:T(8,128)(2,1)S(1)}, bf16[288,1024]{1,0:T(8,128)(2,1)S(1)}, u32[]{:S(2)}, u32[]{:S(2)}) %collective-permute-start.13) | collective-permute-done | bytes 589856 | tf_op jit(solution)/shard_map/ppermute | solution.py:29
  127.9 1.8 collective-permute-start.14
  129.7 10.7 %collective-permute-done.10 = bf16[288,1024]{1,0:T(8,128)(2,1)S(1)} collective-permute-done((bf16[288,1024]{1,0:T(8,128)(2,1)S(1)}, bf16[288,1024]{1,0:T(8,128)(2,1)S(1)}, u32[]{:S(2)}, u32[]{:S(2)}) %collective-permute-start.10) | collective-permute-done | bytes 589856 | tf_op jit(solution)/shard_map/ppermute | solution.py:29
  140.6 2.6 %collective-permute-start.11 = (bf16[288,1024]{1,0:T(8,128)(2,1)S(1)}, bf16[288,1024]{1,0:T(8,128)(2,1)S(1)}, u32[]{:S(2)}, u32[]{:S(2)}) collective-permute-start(bf16[288,1024]{1,0:T(8,128)(2,1)S(1)} %fusion.19), channel_id=1, source_target_pairs={{0,16},{2,18},{4,20},{6,22},{8,24},{10,26},{12,28},{14,30},{16,0},... | collective-permute-start | bytes 1769480 | tf_op jit(solution)/shard_map/ppermute | solution.py:29
  143.2 6.0 %fusion.11 = (f32[2304]{0:T(1024)S(1)}, f32[384,2304]{1,0:T(8,128)}) fusion(bf16[384,2304]{1,0:T(8,128)(2,1)S(1)} %copy-done.1, bf16[384,2304]{1,0:T(8,128)(2,1)} %collective-permute-done.5, f32[384]{0:T(512)S(1)} %add_rsqrt_fusion, f32[384]{0:T(512)S(1)} %add_multiply_fusion, f32[2304]{0:T(1024)S(1)} %get-tuple-element.14, ...), kind=kOutput, calls=%fused_computation.11 | convolution fusion | flops 1820784384 | bytes 12608516 | tf_op jit(solution)/shard_map/dot_general | solution.py:117
  150.4 1.5 collective-permute-start.19
  151.9 2.2 %collective-permute-done.19 = f32[2304]{0:T(1024)S(1)} collective-permute-done((f32[2304]{0:T(1024)S(1)}, f32[2304]{0:T(1024)S(1)}, u32[]{:S(2)}, u32[]{:S(2)}) %collective-permute-start.19) | collective-permute-done | bytes 9248 | tf_op jit(solution)/shard_map/ppermute | solution.py:29
  154.1 2.4 %collective-permute-start.22 = (f32[2304]{0:T(1024)S(1)}, f32[2304]{0:T(1024)S(1)}, u32[]{:S(2)}, u32[]{:S(2)}) collective-permute-start(f32[2304]{0:T(1024)S(1)} %add.255), channel_id=1, source_target_pairs={{0,24},{2,26},{4,28},{6,30},{8,0},{10,2},{12,4},{14,6},{16,8},{18,... | collective-permute-start | bytes 27656 | tf_op jit(solution)/shard_map/ppermute | solution.py:29
  156.5 13.7 %collective-permute-done.22 = f32[2304]{0:T(1024)S(1)} collective-permute-done((f32[2304]{0:T(1024)S(1)}, f32[2304]{0:T(1024)S(1)}, u32[]{:S(2)}, u32[]{:S(2)}) %collective-permute-start.22) | collective-permute-done | bytes 9248 | tf_op jit(solution)/shard_map/ppermute | solution.py:29
  170.9 4.7 %collective-permute-done.20 = f32[2304]{0:T(1024)S(1)} collective-permute-done((f32[2304]{0:T(1024)S(1)}, f32[2304]{0:T(1024)S(1)}, u32[]{:S(2)}, u32[]{:S(2)}) %collective-permute-start.20) | collective-permute-done | bytes 9248 | tf_op jit(solution)/shard_map/ppermute | solution.py:29
  175.6 4.6 %collective-permute-done.21 = f32[2304]{0:T(1024)S(1)} collective-permute-done((f32[2304]{0:T(1024)S(1)}, f32[2304]{0:T(1024)S(1)}, u32[]{:S(2)}, u32[]{:S(2)}) %collective-permute-start.21) | collective-permute-done | bytes 9248 | tf_op jit(solution)/shard_map/ppermute | solution.py:29
  180.8 1.5 fusion.22
  (72 shorter events, 17.5 us)
Async XLA Ops:
  0.6 6.7 %copy-start.1 = (bf16[384,2304]{1,0:T(8,128)(2,1)S(1)}, bf16[384,2304]{1,0:T(8,128)(2,1)}, u32[]{:S(2)}) copy-start(bf16[384,2304]{1,0:T(8,128)(2,1)} %param.4) | copy-start | bytes 5308420
  0.6 5.1 %copy-start.2 = (f32[4608]{0:T(1024)S(1)}, f32[4608]{0:T(1024)}, u32[]{:S(2)}) copy-start(f32[4608]{0:T(1024)} %param.5) | copy-start | bytes 55300
  2.7 4.6 %collective-permute-start = (f32[384]{0:T(512)S(1)}, f32[384]{0:T(512)S(1)}, u32[]{:S(2)}, u32[]{:S(2)}) collective-permute-start(f32[384]{0:T(512)S(1)} %fusion.12), channel_id=1, source_target_pairs={{0,1},{1,0},{2,3},{3,2},{4,5},{5,4},{6,7},{7,6},{8,9},{9,8},{10,11... | collective-permute-start | bytes 4616 | tf_op jit(solution)/shard_map/ppermute | solution.py:19
  7.4 40.3 %copy-start = (bf16[4608,1024]{1,0:T(8,128)(2,1)S(1)}, bf16[4608,1024]{1,0:T(8,128)(2,1)}, u32[]{:S(2)}) copy-start(bf16[4608,1024]{1,0:T(8,128)(2,1)} %param.6) | copy-start | bytes 28311556
  7.6 16.3 %collective-permute-start.1 = (bf16[128,2304]{1,0:T(8,128)(2,1)S(1)}, bf16[128,2304]{1,0:T(8,128)(2,1)S(1)}, u32[]{:S(2)}, u32[]{:S(2)}) collective-permute-start(bf16[128,2304]{1,0:T(8,128)(2,1)S(1)} %get-tuple-element.9), channel_id=1, source_target_pairs={{0,1},{1,0},{2,3},{3,2},{4,5},{5,4},{6,7},{7,6},{8,9},{9,8},{10,11... | collective-permute-start | bytes 1769480 | tf_op jit(solution)/shard_map/ppermute | solution.py:19
  9.7 26.9 %collective-permute-start.3 = (bf16[128,2304]{1,0:T(8,128)(2,1)S(1)}, bf16[128,2304]{1,0:T(8,128)(2,1)S(1)}, u32[]{:S(2)}, u32[]{:S(2)}) collective-permute-start(bf16[128,2304]{1,0:T(8,128)(2,1)S(1)} %get-tuple-element.11), channel_id=1, source_target_pairs={{0,1},{1,0},{2,3},{3,2},{4,5},{5,4},{6,7},{7,6},{8,9},{9,8},{10,11... | collective-permute-start | bytes 1769480 | tf_op jit(solution)/shard_map/ppermute | solution.py:19
  9.8 37.4 %collective-permute-start.2 = (bf16[128,2304]{1,0:T(8,128)(2,1)S(1)}, bf16[128,2304]{1,0:T(8,128)(2,1)S(1)}, u32[]{:S(2)}, u32[]{:S(2)}) collective-permute-start(bf16[128,2304]{1,0:T(8,128)(2,1)S(1)} %get-tuple-element.12), channel_id=1, source_target_pairs={{0,1},{1,0},{2,3},{3,2},{4,5},{5,4},{6,7},{7,6},{8,9},{9,8},{10,11... | collective-permute-start | bytes 1769480 | tf_op jit(solution)/shard_map/ppermute | solution.py:19
  52.9 3.7 %copy-start.3 = (s32[384]{0:T(512)S(1)}, s32[384]{0:T(512)}, u32[]{:S(2)}) copy-start(s32[384]{0:T(512)} %param.7) | copy-start | bytes 4612
  52.9 3.7 %collective-permute-start.4 = (f32[2,384]{1,0:T(2,128)S(1)}, f32[2,384]{1,0:T(2,128)S(1)}, u32[]{:S(2)}, u32[]{:S(2)}) collective-permute-start(f32[2,384]{1,0:T(2,128)S(1)} %pad_maximum_fusion.2), channel_id=1, source_target_pairs={{0,1},{1,0},{2,3},{3,2},{4,5},{5,4},{6,7},{7,6},{8,9},{9,8},{10,11... | collective-permute-start | bytes 9224 | tf_op jit(solution)/shard_map/ppermute | solution.py:19
  60.5 82.7 %collective-permute-start.5 = (bf16[384,2304]{1,0:T(8,128)(2,1)}, bf16[384,2304]{1,0:T(8,128)(2,1)}, u32[]{:S(2)}, u32[]{:S(2)}) collective-permute-start(bf16[384,2304]{1,0:T(8,128)(2,1)} %fusion.6), channel_id=1, source_target_pairs={{0,1},{1,0},{2,3},{3,2},{4,5},{5,4},{6,7},{7,6},{8,9},{9,8},{10,11... | collective-permute-start | bytes 5308424 | tf_op jit(solution)/shard_map/ppermute | solution.py:19
  62.3 36.0 %collective-permute-start.6 = (f32[384]{0:T(512)S(1)}, f32[384]{0:T(512)S(1)}, u32[]{:S(2)}, u32[]{:S(2)}) collective-permute-start(f32[384]{0:T(512)S(1)} %get-tuple-element.5), channel_id=1, source_target_pairs={{0,1},{1,0},{2,3},{3,2},{4,5},{5,4},{6,7},{7,6},{8,9},{9,8},{10,11... | collective-permute-start | bytes 4616 | tf_op jit(solution)/shard_map/ppermute | solution.py:19
  64.2 34.1 %collective-permute-start.15 = (bf16[2,288,1024]{2,1,0:T(8,128)(2,1)S(1)}, bf16[2,288,1024]{2,1,0:T(8,128)(2,1)S(1)}, u32[]{:S(2)}, u32[]{:S(2)}) collective-permute-start(bf16[2,288,1024]{2,1,0:T(8,128)(2,1)S(1)} %fusion.16), channel_id=1, source_target_pairs={{0,2},{2,0},{4,6},{6,4},{8,10},{10,8},{12,14},{14,12},{16,18},{18,... | collective-permute-start | bytes 3538952 | tf_op jit(solution)/shard_map/ppermute | solution.py:29
  65.9 34.5 %collective-permute-start.12 = (bf16[2,288,1024]{2,1,0:T(8,128)(2,1)S(1)}, bf16[2,288,1024]{2,1,0:T(8,128)(2,1)S(1)}, u32[]{:S(2)}, u32[]{:S(2)}) collective-permute-start(bf16[2,288,1024]{2,1,0:T(8,128)(2,1)S(1)} %fusion.15), channel_id=1, source_target_pairs={{0,2},{2,0},{4,6},{6,4},{8,10},{10,8},{12,14},{14,12},{16,18},{18,... | collective-permute-start | bytes 3538952 | tf_op jit(solution)/shard_map/ppermute | solution.py:29
  68.1 33.7 %collective-permute-start.9 = (bf16[2,288,1024]{2,1,0:T(8,128)(2,1)S(1)}, bf16[2,288,1024]{2,1,0:T(8,128)(2,1)S(1)}, u32[]{:S(2)}, u32[]{:S(2)}) collective-permute-start(bf16[2,288,1024]{2,1,0:T(8,128)(2,1)S(1)} %fusion.14), channel_id=1, source_target_pairs={{0,2},{2,0},{4,6},{6,4},{8,10},{10,8},{12,14},{14,12},{16,18},{18,... | collective-permute-start | bytes 3538952 | tf_op jit(solution)/shard_map/ppermute | solution.py:29
  98.3 5.6 %collective-permute-start.7 = (bf16[2,288,1024]{2,1,0:T(8,128)(2,1)S(1)}, bf16[2,288,1024]{2,1,0:T(8,128)(2,1)S(1)}, u32[]{:S(2)}, u32[]{:S(2)}) collective-permute-start(bf16[2,288,1024]{2,1,0:T(8,128)(2,1)S(1)} %fusion.13), channel_id=1, source_target_pairs={{0,2},{2,0},{4,6},{6,4},{8,10},{10,8},{12,14},{14,12},{16,18},{18,... | collective-permute-start | bytes 3538952 | tf_op jit(solution)/shard_map/ppermute | solution.py:29
  98.9 16.2 %collective-permute-start.16 = (bf16[288,1024]{1,0:T(8,128)(2,1)S(1)}, bf16[288,1024]{1,0:T(8,128)(2,1)S(1)}, u32[]{:S(2)}, u32[]{:S(2)}) collective-permute-start(bf16[288,1024]{1,0:T(8,128)(2,1)S(1)} %fusion.40), channel_id=1, source_target_pairs={{0,4},{2,6},{4,0},{6,2},{8,12},{10,14},{12,8},{14,10},{16,20},{18,... | collective-permute-start | bytes 1769480 | tf_op jit(solution)/shard_map/ppermute | solution.py:29
  101.1 26.7 %collective-permute-start.13 = (bf16[288,1024]{1,0:T(8,128)(2,1)S(1)}, bf16[288,1024]{1,0:T(8,128)(2,1)S(1)}, u32[]{:S(2)}, u32[]{:S(2)}) collective-permute-start(bf16[288,1024]{1,0:T(8,128)(2,1)S(1)} %fusion.39), channel_id=1, source_target_pairs={{0,4},{2,6},{4,0},{6,2},{8,12},{10,14},{12,8},{14,10},{16,20},{18,... | collective-permute-start | bytes 1769480 | tf_op jit(solution)/shard_map/ppermute | solution.py:29
  102.4 38.0 %collective-permute-start.10 = (bf16[288,1024]{1,0:T(8,128)(2,1)S(1)}, bf16[288,1024]{1,0:T(8,128)(2,1)S(1)}, u32[]{:S(2)}, u32[]{:S(2)}) collective-permute-start(bf16[288,1024]{1,0:T(8,128)(2,1)S(1)} %fusion.38), channel_id=1, source_target_pairs={{0,4},{2,6},{4,0},{6,2},{8,12},{10,14},{12,8},{14,10},{16,20},{18,... | collective-permute-start | bytes 1769480 | tf_op jit(solution)/shard_map/ppermute | solution.py:29
  104.5 76.3 %collective-permute-start.8 = (bf16[288,1024]{1,0:T(8,128)(2,1)S(1)}, bf16[288,1024]{1,0:T(8,128)(2,1)S(1)}, u32[]{:S(2)}, u32[]{:S(2)}) collective-permute-start(bf16[288,1024]{1,0:T(8,128)(2,1)S(1)} %fusion.37), channel_id=1, source_target_pairs={{0,4},{2,6},{4,0},{6,2},{8,12},{10,14},{12,8},{14,10},{16,20},{18,... | collective-permute-start | bytes 1769480 | tf_op jit(solution)/shard_map/ppermute | solution.py:29
  115.3 65.5 %collective-permute-start.17 = (bf16[288,1024]{1,0:T(8,128)(2,1)S(1)}, bf16[288,1024]{1,0:T(8,128)(2,1)S(1)}, u32[]{:S(2)}, u32[]{:S(2)}) collective-permute-start(bf16[288,1024]{1,0:T(8,128)(2,1)S(1)} %fusion.17), channel_id=1, source_target_pairs={{0,24},{2,26},{4,28},{6,30},{8,0},{10,2},{12,4},{14,6},{16,8},{18,... | collective-permute-start | bytes 1769480 | tf_op jit(solution)/shard_map/ppermute | solution.py:29
  127.9 52.9 %collective-permute-start.14 = (bf16[288,1024]{1,0:T(8,128)(2,1)S(1)}, bf16[288,1024]{1,0:T(8,128)(2,1)S(1)}, u32[]{:S(2)}, u32[]{:S(2)}) collective-permute-start(bf16[288,1024]{1,0:T(8,128)(2,1)S(1)} %fusion.18), channel_id=1, source_target_pairs={{0,8},{2,10},{4,12},{6,14},{8,16},{10,18},{12,20},{14,22},{16,24},... | collective-permute-start | bytes 1769480 | tf_op jit(solution)/shard_map/ppermute | solution.py:29
  140.6 40.2 %collective-permute-start.11 = (bf16[288,1024]{1,0:T(8,128)(2,1)S(1)}, bf16[288,1024]{1,0:T(8,128)(2,1)S(1)}, u32[]{:S(2)}, u32[]{:S(2)}) collective-permute-start(bf16[288,1024]{1,0:T(8,128)(2,1)S(1)} %fusion.19), channel_id=1, source_target_pairs={{0,16},{2,18},{4,20},{6,22},{8,24},{10,26},{12,28},{14,30},{16,0},... | collective-permute-start | bytes 1769480 | tf_op jit(solution)/shard_map/ppermute | solution.py:29
  149.2 1.2 collective-permute-start.18
  150.4 3.7 %collective-permute-start.19 = (f32[2304]{0:T(1024)S(1)}, f32[2304]{0:T(1024)S(1)}, u32[]{:S(2)}, u32[]{:S(2)}) collective-permute-start(f32[2304]{0:T(1024)S(1)} %add.254), channel_id=1, source_target_pairs={{0,4},{2,6},{4,0},{6,2},{8,12},{10,14},{12,8},{14,10},{16,20},{18,... | collective-permute-start | bytes 27656 | tf_op jit(solution)/shard_map/ppermute | solution.py:29
  154.1 16.1 %collective-permute-start.22 = (f32[2304]{0:T(1024)S(1)}, f32[2304]{0:T(1024)S(1)}, u32[]{:S(2)}, u32[]{:S(2)}) collective-permute-start(f32[2304]{0:T(1024)S(1)} %add.255), channel_id=1, source_target_pairs={{0,24},{2,26},{4,28},{6,30},{8,0},{10,2},{12,4},{14,6},{16,8},{18,... | collective-permute-start | bytes 27656 | tf_op jit(solution)/shard_map/ppermute | solution.py:29
  170.1 5.5 %collective-permute-start.20 = (f32[2304]{0:T(1024)S(1)}, f32[2304]{0:T(1024)S(1)}, u32[]{:S(2)}, u32[]{:S(2)}) collective-permute-start(f32[2304]{0:T(1024)S(1)} %add.255), channel_id=1, source_target_pairs={{0,8},{2,10},{4,12},{6,14},{8,16},{10,18},{12,20},{14,22},{16,24},... | collective-permute-start | bytes 27656 | tf_op jit(solution)/shard_map/ppermute | solution.py:29
  175.6 4.6 %collective-permute-start.21 = (f32[2304]{0:T(1024)S(1)}, f32[2304]{0:T(1024)S(1)}, u32[]{:S(2)}, u32[]{:S(2)}) collective-permute-start(f32[2304]{0:T(1024)S(1)} %add.255), channel_id=1, source_target_pairs={{0,16},{2,18},{4,20},{6,22},{8,24},{10,26},{12,28},{14,30},{16,0},... | collective-permute-start | bytes 27656 | tf_op jit(solution)/shard_map/ppermute | solution.py:29

commit v2 on v1

--- a/solution.py
+++ b/solution.py
@@ -6,6 +6,10 @@
 epsilon = 1e-06
 bf16 = jnp.bfloat16
 f32 = jnp.float32
+
+
+def after(x, dep):
+    return lax.optimization_barrier((x, dep))[0]
 
 
 def make(mesh):
@@ -26,6 +30,13 @@
                     src = (a * nb + b) * nc + c
                     dst = (((a + da) % na) * nb + (b + db) % nb) * nc + (c + dc) % nc
                     pairs.append((src, dst))
+        return lax.ppermute(x, "dp", pairs)
+
+    def dp_to(x, move):
+        pairs = []
+        for i in range(ndp):
+            a, rest = i // (nb * nc), i % (nb * nc)
+            pairs.append((i, move(a) * nb * nc + rest))
         return lax.ppermute(x, "dp", pairs)
 
     def shards(h, gain, head, targets):
@@ -83,11 +94,6 @@
         exact = jnp.exp(logits - log_total[:, None]) - onehot
         dlogits = exact.astype(bf16)
         dot_own = jnp.sum(dlogits.astype(f32) * logits, axis=1)
-        dot_all = dot_own
-        for k in range(1, nt):
-            dot_all = dot_all + shift_tensor(dot_own, k)
-        row_dot = dot_all / width
-
         arrived = []
         for k in range(1, nt):
             part = lax.dot_general(dlogits, w_block(k), (((1,), (1,)), ((), ())),
@@ -96,10 +102,7 @@
 
         block = width // na
         small = width // ndp
-        order = list(range(na // 2, 0, -1)) + list(range(na // 2 + 1, na)) + [0]
-        pieces = []
-        for k in order:
-            to = (a + k) % na
+        def halves(to):
             cut = lax.dynamic_slice_in_dim(normed, to * block, block, axis=1)
             prod = lax.dot_general(cut, dlogits, (((0,), (0,)), ((), ())),
                                    preferred_element_type=f32)
@@ -109,10 +112,42 @@
             keep = keep + dp_shift(away, 0, 0, 1).astype(f32)
             mine = lax.dynamic_index_in_dim(keep, b, axis=0, keepdims=False)
             other = lax.dynamic_index_in_dim(keep, 1 - b, axis=0, keepdims=False).astype(bf16)
-            mine = mine + dp_shift(other, 0, 1, 0).astype(f32)
-            if k:
-                mine = dp_shift(mine.astype(bf16), k, 0, 0).astype(f32)
-            pieces.append(mine)
+            return mine, dp_shift(other, 0, 1, 0)
+
+        def partial(to):
+            mine, other = halves(to)
+            return mine + other.astype(f32)
+
+        if na == 4:
+            near = a + 1 - 2 * (a % 2)
+            first = partial(na - 1 - near).astype(bf16)
+            first_in = dp_to(first, lambda i: i ^ 1)
+            mine, other = halves(na - 1 - a)
+            other = after(other, first)
+            second = (mine + other.astype(f32) + first_in.astype(f32)).astype(bf16)
+            second_in = dp_to(second, lambda i: na - 1 - i)
+            arrived = [after(p, second) for p in arrived]
+            mine, other = halves(near)
+            other = after(other, second)
+            third = (mine + other.astype(f32)).astype(bf16)
+            third_in = dp_to(third, lambda i: i ^ 1)
+            mine, other = halves(a)
+            other = after(other, third)
+            grad_head = (mine + other.astype(f32) + third_in.astype(f32)
+                         + second_in.astype(f32))
+        else:
+            grad_head = 0.0
+            for k in list(range(na // 2, 0, -1)) + list(range(na // 2 + 1, na)):
+                got_block = dp_shift(partial((a + k) % na).astype(bf16), k, 0, 0)
+                grad_head = grad_head + got_block.astype(f32)
+            grad_head = grad_head + partial(a)
+
+        if arrived:
+            dot_own = after(dot_own, arrived)
+        dot_all = dot_own
+        for k in range(1, nt):
+            dot_all = dot_all + shift_tensor(dot_own, k)
+        row_dot = dot_all / width
 
         grad = lax.dot_general(dlogits, w_block(0), (((1,), (1,)), ((), ())),
                                preferred_element_type=f32)
@@ -124,9 +159,6 @@
         gain_grad = gain_grad + dp_shift(gain_grad, 0, 0, 1)
         gain_grad = gain_grad + dp_shift(gain_grad, 0, 1, 0)
         gain_grad = gain_grad + sum(dp_shift(gain_grad, k, 0, 0) for k in range(1, na))
-        grad_head = pieces[-1]
-        for p in pieces[:-1]:
-            grad_head = grad_head + p
         return hidden, grad_head, gain_grad
 
     return shards

time: 182 us -> 136 us (0.75)
  waiting for transfers between devices: 122 us -> 69.1 us
  other arithmetic: 9.44 us -> 13.3 us
  starting transfers between devices: 28.6 us -> 30.9 us
    ppermute x16 -> x13, waiting for transfers between devices: 55.8 us -> 18.7 us  [dp_shift(): return lax.ppermute(x, 'dp', pairs)]
    ppermute x7, waiting for transfers between devices: 66.4 us -> 49.3 us  [shift_tensor(): return lax.ppermute(x, 'tensor', [(i, (i + k) % nt) for i in range(nt)])]
    ppermute x0 -> x3, starting transfers between devices: none -> 7.32 us  [dp_to(): return lax.ppermute(x, 'dp', pairs)]
    ppermute x16 -> x13, starting transfers between devices: 17.6 us -> 11.7 us  [dp_shift(): return lax.ppermute(x, 'dp', pairs)]
    add x5, other arithmetic: 3.67 us -> 7.19 us  [the longest x4 5.82 us: halves(): keep = keep + dp_shift(away, 0, 0, 1).astype(f32)]
  transfers between devices with their start and end apart: 23 -> 23, of which waited for: 14 -> 14; matrix products, arithmetic and copies ran while one was open for 9% -> 17% of each run, Pallas kernels for 0% -> 0%
where the time goes in v2:
time: 136 us; the launch traced here: 135 us
  waiting for transfers between devices  69.1 us (51%)
  starting transfers between devices  30.9 us (23%)
  matrix products  19.7 us (14%)
  other arithmetic  13.3 us (10%)
  local copies, waits for them, and re-layouts  1.47 us (1%)
    ppermute x7, waiting for transfers between devices, shift_tensor(): return lax.ppermute(x, 'tensor', [(i, (i + k) % nt) for i in range(nt)])  49.3 us
    ppermute x13, waiting for transfers between devices, dp_shift(): return lax.ppermute(x, 'dp', pairs)  18.7 us
    ppermute x7, starting transfers between devices, shift_tensor(): return lax.ppermute(x, 'tensor', [(i, (i + k) % nt) for i in range(nt)])  12 us
    ppermute x13, starting transfers between devices, dp_shift(): return lax.ppermute(x, 'dp', pairs)  11.7 us
    ppermute x3, starting transfers between devices, dp_to(): return lax.ppermute(x, 'dp', pairs)  7.32 us
    dot_general x1, matrix products, shards(): lax.dot_general(dlogits, w_block(0), (((1,), (1,)), ((), ())), preferred_...  6.01 us
    add x4, other arithmetic, halves(): keep = keep + dp_shift(away, 0, 0, 1).astype(f32)  5.82 us
    dot_general x4, matrix products, halves(): lax.dot_general(cut, dlogits, (((0,), (0,)), ((), ())), preferred_element...  5.77 us
  transfers between devices with their start and end apart: 23, of which 14 were waited for; matrix products, arithmetic and copies ran while one was open for 17% of the time, Pallas kernels for 0%

profile of v2, /device:TPU:0, one launch (start us, length us, event | category | flops | bytes accessed | tf_op | source)
XLA Modules:
  0.0 135.4 jit_solution(3234275480983272251)
XLA Ops:
  0.6 2.0 %fusion.12 = f32[384]{0:T(512)S(1)} fusion(bf16[384,2304]{1,0:T(8,128)(2,1)} %param.4), kind=kLoop, calls=%fused_computation.12 | loop fusion | flops 2653824 | bytes 1771008 | tf_op jit(solution)/shard_map/reduce_sum | solution.py:49
  2.7 3.0 %collective-permute-start = (f32[384]{0:T(512)S(1)}, f32[384]{0:T(512)S(1)}, u32[]{:S(2)}, u32[]{:S(2)}) collective-permute-start(f32[384]{0:T(512)S(1)} %fusion.12), channel_id=1, source_target_pairs={{0,1},{1,0},{2,3},{3,2},{4,5},{5,4},{6,7},{7,6},{8,9},{9,8},{10,11... | collective-permute-start | bytes 4616 | tf_op jit(solution)/shard_map/ppermute | solution.py:23
  5.8 1.5 %collective-permute-done = f32[384]{0:T(512)S(1)} collective-permute-done((f32[384]{0:T(512)S(1)}, f32[384]{0:T(512)S(1)}, u32[]{:S(2)}, u32[]{:S(2)}) %collective-permute-start) | collective-permute-done | bytes 1568 | tf_op jit(solution)/shard_map/ppermute | solution.py:23
  7.6 2.1 %collective-permute-start.1 = (bf16[128,2304]{1,0:T(8,128)(2,1)S(1)}, bf16[128,2304]{1,0:T(8,128)(2,1)S(1)}, u32[]{:S(2)}, u32[]{:S(2)}) collective-permute-start(bf16[128,2304]{1,0:T(8,128)(2,1)S(1)} %get-tuple-element.19), channel_id=1, source_target_pairs={{0,1},{1,0},{2,3},{3,2},{4,5},{5,4},{6,7},{7,6},{8,9},{9,8},{10,11... | collective-permute-start | bytes 1769480 | tf_op jit(solution)/shard_map/ppermute | solution.py:23
  9.8 1.9 %collective-permute-start.3 = (bf16[128,2304]{1,0:T(8,128)(2,1)S(1)}, bf16[128,2304]{1,0:T(8,128)(2,1)S(1)}, u32[]{:S(2)}, u32[]{:S(2)}) collective-permute-start(bf16[128,2304]{1,0:T(8,128)(2,1)S(1)} %get-tuple-element.21), channel_id=1, source_target_pairs={{0,1},{1,0},{2,3},{3,2},{4,5},{5,4},{6,7},{7,6},{8,9},{9,8},{10,11... | collective-permute-start | bytes 1769480 | tf_op jit(solution)/shard_map/ppermute | solution.py:23
  12.3 11.6 %collective-permute-done.1 = bf16[128,2304]{1,0:T(8,128)(2,1)S(1)} collective-permute-done((bf16[128,2304]{1,0:T(8,128)(2,1)S(1)}, bf16[128,2304]{1,0:T(8,128)(2,1)S(1)}, u32[]{:S(2)}, u32[]{:S(2)}) %collective-permute-start.1) | collective-permute-done | bytes 589856 | tf_op jit(solution)/shard_map/ppermute | solution.py:23
  24.0 12.6 %collective-permute-done.2 = bf16[128,2304]{1,0:T(8,128)(2,1)S(1)} collective-permute-done((bf16[128,2304]{1,0:T(8,128)(2,1)S(1)}, bf16[128,2304]{1,0:T(8,128)(2,1)S(1)}, u32[]{:S(2)}, u32[]{:S(2)}) %collective-permute-start.2) | collective-permute-done | bytes 589856 | tf_op jit(solution)/shard_map/ppermute | solution.py:23
  36.6 10.6 %collective-permute-done.3 = bf16[128,2304]{1,0:T(8,128)(2,1)S(1)} collective-permute-done((bf16[128,2304]{1,0:T(8,128)(2,1)S(1)}, bf16[128,2304]{1,0:T(8,128)(2,1)S(1)}, u32[]{:S(2)}, u32[]{:S(2)}) %collective-permute-start.3) | collective-permute-done | bytes 589856 | tf_op jit(solution)/shard_map/ppermute | solution.py:23
  47.7 1.6 %fusion.53 = f32[128,1024]{1,0:T(8,128)S(1)} fusion(bf16[128,4608]{1,0:T(8,128)(2,1)S(1)} %get-tuple-element.25, bf16[4608,1024]{1,0:T(8,128)(2,1)S(1)} %copy-done), kind=kOutput, calls=%fused_computation.90 | convolution fusion | flops 1207959552 | bytes 11141120 | tf_op jit(solution)/shard_map/dot_general | solution.py:79
  49.2 1.6 %fusion.54 = f32[128,1024]{1,0:T(8,128)S(1)} fusion(bf16[128,4608]{1,0:T(8,128)(2,1)S(1)} %get-tuple-element.27, bf16[4608,1024]{1,0:T(8,128)(2,1)S(1)} %copy-done), kind=kOutput, calls=%fused_computation.91 | convolution fusion | flops 1207959552 | bytes 11141120 | tf_op jit(solution)/shard_map/dot_general | solution.py:79
  50.8 1.6 %fusion.55 = f32[128,1024]{1,0:T(8,128)S(1)} fusion(bf16[128,4608]{1,0:T(8,128)(2,1)S(1)} %get-tuple-element.26, bf16[4608,1024]{1,0:T(8,128)(2,1)S(1)} %copy-done), kind=kOutput, calls=%fused_computation.92 | convolution fusion | flops 1207959552 | bytes 11141120 | tf_op jit(solution)/shard_map/dot_general | solution.py:79
  53.0 1.8 %collective-permute-start.4 = (f32[2,384]{1,0:T(2,128)S(1)}, f32[2,384]{1,0:T(2,128)S(1)}, u32[]{:S(2)}, u32[]{:S(2)}) collective-permute-start(f32[2,384]{1,0:T(2,128)S(1)} %pad_maximum_fusion.2), channel_id=1, source_target_pairs={{0,1},{1,0},{2,3},{3,2},{4,5},{5,4},{6,7},{7,6},{8,9},{9,8},{10,11... | collective-permute-start | bytes 9224 | tf_op jit(solution)/shard_map/ppermute | solution.py:23
  62.9 1.4 %fusion.23 = f32[1152,1024]{1,0:T(8,128)S(1)} fusion(bf16[384,1024]{1,0:T(8,128)(2,1)S(1)} %get-tuple-element.16, bf16[384,4608]{1,0:T(8,128)(2,1)S(1)} %pad_maximum_fusion, s32[]{:T(128)S(6)} %select_n.135), kind=kOutput, calls=%fused_computation.51 | convolution fusion | flops 905969664 | bytes 6389764 | tf_op jit(solution)/shard_map/dot_general | solution.py:107
  65.6 1.8 %collective-permute-start.9 = (bf16[288,1024]{1,0:T(8,128)(2,1)S(1)}, bf16[288,1024]{1,0:T(8,128)(2,1)S(1)}, u32[]{:S(2)}, u32[]{:S(2)}) collective-permute-start(bf16[288,1024]{1,0:T(8,128)(2,1)S(1)} %fusion.38), channel_id=1, source_target_pairs={{0,4},{2,6},{4,0},{6,2},{8,12},{10,14},{12,8},{14,10},{16,20},{18,... | collective-permute-start | bytes 1769480 | tf_op jit(solution)/shard_map/ppermute | solution.py:33
  67.3 3.3 %fusion.6 = bf16[384,2304]{1,0:T(8,128)(2,1)} fusion(bf16[384,1024]{1,0:T(8,128)(2,1)S(1)} %get-tuple-element.16, bf16[4608,1024]{1,0:T(8,128)(2,1)S(1)} %copy-done, s32[]{:T(128)S(6)} %select_n.122), kind=kOutput, calls=%fused_computation.8 | convolution fusion | flops 1812824064 | bytes 7274500 | tf_op jit(solution)/shard_map/dot_general | solution.py:99
  70.6 1.5 %collective-permute-start.5 = (bf16[384,2304]{1,0:T(8,128)(2,1)}, bf16[384,2304]{1,0:T(8,128)(2,1)S(1)}, u32[]{:S(2)}, u32[]{:S(2)}) collective-permute-start(bf16[384,2304]{1,0:T(8,128)(2,1)} %fusion.6), channel_id=1, source_target_pairs={{0,1},{1,0},{2,3},{3,2},{4,5},{5,4},{6,7},{7,6},{8,9},{9,8},{10,11... | collective-permute-start | bytes 5308424 | tf_op jit(solution)/shard_map/ppermute | solution.py:23
  72.1 1.8 %bitcast_add_fusion.3 = f32[2,288,1024]{2,1,0:T(8,128)S(1)} fusion(bf16[2,288,1024]{2,1,0:T(8,128)(2,1)} %collective-permute-done.6, f32[2,2,288,1024]{3,2,1,0:T(8,128)S(1)} %bitcast.81, s32[]{:T(128)S(6)} %select_n.126), kind=kLoop, calls=%fused_computation.22 | loop fusion | flops 1179648 | bytes 5898244 | tf_op jit(solution)/shard_map/add | solution.py:112
  74.6 7.2 %collective-permute-done.9 = bf16[288,1024]{1,0:T(8,128)(2,1)S(1)} collective-permute-done((bf16[288,1024]{1,0:T(8,128)(2,1)S(1)}, bf16[288,1024]{1,0:T(8,128)(2,1)S(1)}, u32[]{:S(2)}, u32[]{:S(2)}) %collective-permute-start.9) | collective-permute-done | bytes 589856 | tf_op jit(solution)/shard_map/ppermute | solution.py:33
  82.0 1.9 %collective-permute-start.10 = (bf16[288,1024]{1,0:T(8,128)(2,1)S(1)}, bf16[288,1024]{1,0:T(8,128)(2,1)S(1)}, u32[]{:S(2)}, u32[]{:S(2)}) collective-permute-start(bf16[288,1024]{1,0:T(8,128)(2,1)S(1)} %fusion.20), channel_id=1, source_target_pairs={{0,8},{2,10},{4,12},{6,14},{8,0},{10,2},{12,4},{14,6},{16,24},{18,... | collective-permute-start | bytes 1769480 | tf_op jit(solution)/shard_map/ppermute | solution.py:40
  83.9 1.8 %bitcast_add_fusion = f32[2,288,1024]{2,1,0:T(8,128)S(1)} fusion(bf16[2,288,1024]{2,1,0:T(8,128)(2,1)} %collective-permute-done.14, f32[2,2,288,1024]{3,2,1,0:T(8,128)S(1)} %bitcast.79, s32[]{:T(128)S(6)} %select_n.126), kind=kLoop, calls=%fused_computation.19 | loop fusion | flops 1179648 | bytes 5898244 | tf_op jit(solution)/shard_map/add | solution.py:112
  85.8 1.5 %collective-permute-start.15 = (bf16[288,1024]{1,0:T(8,128)(2,1)S(1)}, bf16[288,1024]{1,0:T(8,128)(2,1)S(1)}, u32[]{:S(2)}, u32[]{:S(2)}) collective-permute-start(bf16[288,1024]{1,0:T(8,128)(2,1)S(1)} %fusion.40), channel_id=1, source_target_pairs={{0,4},{2,6},{4,0},{6,2},{8,12},{10,14},{12,8},{14,10},{16,20},{18,... | collective-permute-start | bytes 1769480 | tf_op jit(solution)/shard_map/ppermute | solution.py:33
  87.4 1.8 %bitcast_add_fusion.1 = f32[2,288,1024]{2,1,0:T(8,128)S(1)} fusion(bf16[2,288,1024]{2,1,0:T(8,128)(2,1)} %collective-permute-done.12, f32[2,2,288,1024]{3,2,1,0:T(8,128)S(1)} %bitcast.77, s32[]{:T(128)S(6)} %select_n.126), kind=kLoop, calls=%fused_computation.20 | loop fusion | flops 1179648 | bytes 5898244 | tf_op jit(solution)/shard_map/add | solution.py:112
  89.9 4.6 %collective-permute-done.7 = bf16[288,1024]{1,0:T(8,128)(2,1)S(1)} collective-permute-done((bf16[288,1024]{1,0:T(8,128)(2,1)S(1)}, bf16[288,1024]{1,0:T(8,128)(2,1)S(1)}, u32[]{:S(2)}, u32[]{:S(2)}) %collective-permute-start.7) | collective-permute-done | bytes 589856 | tf_op jit(solution)/shard_map/ppermute | solution.py:33
  95.9 3.8 %collective-permute-start.17 = (bf16[288,1024]{1,0:T(8,128)(2,1)S(1)}, bf16[288,1024]{1,0:T(8,128)(2,1)S(1)}, u32[]{:S(2)}, u32[]{:S(2)}) collective-permute-start(bf16[288,1024]{1,0:T(8,128)(2,1)S(1)} %fusion.22), channel_id=1, source_target_pairs={{0,24},{2,26},{4,28},{6,30},{8,16},{10,18},{12,20},{14,22},{16,8},... | collective-permute-start | bytes 1769480 | tf_op jit(solution)/shard_map/ppermute | solution.py:40
  99.7 11.3 %collective-permute-done.5 = bf16[384,2304]{1,0:T(8,128)(2,1)S(1)} collective-permute-done((bf16[384,2304]{1,0:T(8,128)(2,1)}, bf16[384,2304]{1,0:T(8,128)(2,1)S(1)}, u32[]{:S(2)}, u32[]{:S(2)}) %collective-permute-start.5) | collective-permute-done | bytes 1769504 | tf_op jit(solution)/shard_map/ppermute | solution.py:23
  111.0 1.5 %collective-permute-start.11 = (f32[384]{0:T(512)S(1)}, f32[384]{0:T(512)S(1)}, u32[]{:S(2)}, u32[]{:S(2)}) collective-permute-start(f32[384]{0:T(512)S(1)} %get-tuple-element.10), channel_id=1, source_target_pairs={{0,1},{1,0},{2,3},{3,2},{4,5},{5,4},{6,7},{7,6},{8,9},{9,8},{10,11... | collective-permute-start | bytes 4616 | tf_op jit(solution)/shard_map/ppermute | solution.py:23
  112.8 1.6 %collective-permute-start.16 = (bf16[288,1024]{1,0:T(8,128)(2,1)S(1)}, bf16[288,1024]{1,0:T(8,128)(2,1)S(1)}, u32[]{:S(2)}, u32[]{:S(2)}) collective-permute-start(bf16[288,1024]{1,0:T(8,128)(2,1)S(1)} %fusion.17), channel_id=1, source_target_pairs={{0,8},{2,10},{4,12},{6,14},{8,0},{10,2},{12,4},{14,6},{16,24},{18,... | collective-permute-start | bytes 1769480 | tf_op jit(solution)/shard_map/ppermute | solution.py:40
  114.6 6.0 %fusion.11 = (f32[2304]{0:T(1024)S(1)}, f32[384,2304]{1,0:T(8,128)}) fusion(bf16[384,2304]{1,0:T(8,128)(2,1)S(1)} %copy-done.1, bf16[384,2304]{1,0:T(8,128)(2,1)} %copy-done.4, f32[384]{0:T(512)S(1)} %add_rsqrt_fusion, f32[384]{0:T(512)S(1)} %add_multiply_fusion, f32[2304]{0:T(1024)S(1)} %get-tuple-element.24, bf16[384,1024]{1,0:T(8,128)(2,1)S(1)} %get-tuple-element.16, ...), kind=kOutput, calls=%fused_computation.11 | convolution fusion | flops 1820784384 | bytes 12608516 | tf_op jit(solution)/shard_map/dot_general | solution.py:152
  122.2 3.4 %collective-permute-done.19 = f32[2304]{0:T(1024)S(1)} collective-permute-done((f32[2304]{0:T(1024)S(1)}, f32[2304]{0:T(1024)S(1)}, u32[]{:S(2)}, u32[]{:S(2)}) %collective-permute-start.19) | collective-permute-done | bytes 9248 | tf_op jit(solution)/shard_map/ppermute | solution.py:33
  125.5 1.6 %collective-permute-start.20 = (f32[2304]{0:T(1024)S(1)}, f32[2304]{0:T(1024)S(1)}, u32[]{:S(2)}, u32[]{:S(2)}) collective-permute-start(f32[2304]{0:T(1024)S(1)} %add.235), channel_id=1, source_target_pairs={{0,8},{2,10},{4,12},{6,14},{8,16},{10,18},{12,20},{14,22},{16,24},... | collective-permute-start | bytes 27656 | tf_op jit(solution)/shard_map/ppermute | solution.py:33
  127.1 2.6 %collective-permute-start.21 = (f32[2304]{0:T(1024)S(1)}, f32[2304]{0:T(1024)S(1)}, u32[]{:S(2)}, u32[]{:S(2)}) collective-permute-start(f32[2304]{0:T(1024)S(1)} %add.235), channel_id=1, source_target_pairs={{0,16},{2,18},{4,20},{6,22},{8,24},{10,26},{12,28},{14,30},{16,0},... | collective-permute-start | bytes 27656 | tf_op jit(solution)/shard_map/ppermute | solution.py:33
  131.7 1.7 %collective-permute-done.22 = f32[2304]{0:T(1024)S(1)} collective-permute-done((f32[2304]{0:T(1024)S(1)}, f32[2304]{0:T(1024)S(1)}, u32[]{:S(2)}, u32[]{:S(2)}) %collective-permute-start.22) | collective-permute-done | bytes 9248 | tf_op jit(solution)/shard_map/ppermute | solution.py:33
  (74 shorter events, 20.5 us)
Async XLA Ops:
  0.6 6.7 %copy-start.1 = (bf16[384,2304]{1,0:T(8,128)(2,1)S(1)}, bf16[384,2304]{1,0:T(8,128)(2,1)}, u32[]{:S(2)}) copy-start(bf16[384,2304]{1,0:T(8,128)(2,1)} %param.4) | copy-start | bytes 5308420
  0.6 5.1 %copy-start.2 = (f32[4608]{0:T(1024)S(1)}, f32[4608]{0:T(1024)}, u32[]{:S(2)}) copy-start(f32[4608]{0:T(1024)} %param.5) | copy-start | bytes 55300
  2.7 4.6 %collective-permute-start = (f32[384]{0:T(512)S(1)}, f32[384]{0:T(512)S(1)}, u32[]{:S(2)}, u32[]{:S(2)}) collective-permute-start(f32[384]{0:T(512)S(1)} %fusion.12), channel_id=1, source_target_pairs={{0,1},{1,0},{2,3},{3,2},{4,5},{5,4},{6,7},{7,6},{8,9},{9,8},{10,11... | collective-permute-start | bytes 4616 | tf_op jit(solution)/shard_map/ppermute | solution.py:23
  7.4 40.3 %copy-start = (bf16[4608,1024]{1,0:T(8,128)(2,1)S(1)}, bf16[4608,1024]{1,0:T(8,128)(2,1)}, u32[]{:S(2)}) copy-start(bf16[4608,1024]{1,0:T(8,128)(2,1)} %param.6) | copy-start | bytes 28311556
  7.6 16.3 %collective-permute-start.1 = (bf16[128,2304]{1,0:T(8,128)(2,1)S(1)}, bf16[128,2304]{1,0:T(8,128)(2,1)S(1)}, u32[]{:S(2)}, u32[]{:S(2)}) collective-permute-start(bf16[128,2304]{1,0:T(8,128)(2,1)S(1)} %get-tuple-element.19), channel_id=1, source_target_pairs={{0,1},{1,0},{2,3},{3,2},{4,5},{5,4},{6,7},{7,6},{8,9},{9,8},{10,11... | collective-permute-start | bytes 1769480 | tf_op jit(solution)/shard_map/ppermute | solution.py:23
  9.7 26.9 %collective-permute-start.2 = (bf16[128,2304]{1,0:T(8,128)(2,1)S(1)}, bf16[128,2304]{1,0:T(8,128)(2,1)S(1)}, u32[]{:S(2)}, u32[]{:S(2)}) collective-permute-start(bf16[128,2304]{1,0:T(8,128)(2,1)S(1)} %get-tuple-element.22), channel_id=1, source_target_pairs={{0,1},{1,0},{2,3},{3,2},{4,5},{5,4},{6,7},{7,6},{8,9},{9,8},{10,11... | collective-permute-start | bytes 1769480 | tf_op jit(solution)/shard_map/ppermute | solution.py:23
  9.8 37.4 %collective-permute-start.3 = (bf16[128,2304]{1,0:T(8,128)(2,1)S(1)}, bf16[128,2304]{1,0:T(8,128)(2,1)S(1)}, u32[]{:S(2)}, u32[]{:S(2)}) collective-permute-start(bf16[128,2304]{1,0:T(8,128)(2,1)S(1)} %get-tuple-element.21), channel_id=1, source_target_pairs={{0,1},{1,0},{2,3},{3,2},{4,5},{5,4},{6,7},{7,6},{8,9},{9,8},{10,11... | collective-permute-start | bytes 1769480 | tf_op jit(solution)/shard_map/ppermute | solution.py:23
  52.9 3.7 %copy-start.3 = (s32[384]{0:T(512)S(1)}, s32[384]{0:T(512)}, u32[]{:S(2)}) copy-start(s32[384]{0:T(512)} %param.7) | copy-start | bytes 4612
  53.0 3.7 %collective-permute-start.4 = (f32[2,384]{1,0:T(2,128)S(1)}, f32[2,384]{1,0:T(2,128)S(1)}, u32[]{:S(2)}, u32[]{:S(2)}) collective-permute-start(f32[2,384]{1,0:T(2,128)S(1)} %pad_maximum_fusion.2), channel_id=1, source_target_pairs={{0,1},{1,0},{2,3},{3,2},{4,5},{5,4},{6,7},{7,6},{8,9},{9,8},{10,11... | collective-permute-start | bytes 9224 | tf_op jit(solution)/shard_map/ppermute | solution.py:23
  58.9 6.2 %collective-permute-start.8 = (bf16[2,288,1024]{2,1,0:T(8,128)(2,1)S(1)}, bf16[2,288,1024]{2,1,0:T(8,128)(2,1)S(1)}, u32[]{:S(2)}, u32[]{:S(2)}) collective-permute-start(bf16[2,288,1024]{2,1,0:T(8,128)(2,1)S(1)} %fusion.14), channel_id=1, source_target_pairs={{0,2},{2,0},{4,6},{6,4},{8,10},{10,8},{12,14},{14,12},{16,18},{18,... | collective-permute-start | bytes 3538952 | tf_op jit(solution)/shard_map/ppermute | solution.py:33
  60.6 11.5 %collective-permute-start.6 = (bf16[2,288,1024]{2,1,0:T(8,128)(2,1)S(1)}, bf16[2,288,1024]{2,1,0:T(8,128)(2,1)}, u32[]{:S(2)}, u32[]{:S(2)}) collective-permute-start(bf16[2,288,1024]{2,1,0:T(8,128)(2,1)S(1)} %fusion.13), channel_id=1, source_target_pairs={{0,2},{2,0},{4,6},{6,4},{8,10},{10,8},{12,14},{14,12},{16,18},{18,... | collective-permute-start | bytes 3538952 | tf_op jit(solution)/shard_map/ppermute | solution.py:33
  62.8 24.6 %collective-permute-start.12 = (bf16[2,288,1024]{2,1,0:T(8,128)(2,1)S(1)}, bf16[2,288,1024]{2,1,0:T(8,128)(2,1)}, u32[]{:S(2)}, u32[]{:S(2)}) collective-permute-start(bf16[2,288,1024]{2,1,0:T(8,128)(2,1)S(1)} %fusion.15), channel_id=1, source_target_pairs={{0,2},{2,0},{4,6},{6,4},{8,10},{10,8},{12,14},{14,12},{16,18},{18,... | collective-permute-start | bytes 3538952 | tf_op jit(solution)/shard_map/ppermute | solution.py:33
  64.5 19.4 %collective-permute-start.14 = (bf16[2,288,1024]{2,1,0:T(8,128)(2,1)S(1)}, bf16[2,288,1024]{2,1,0:T(8,128)(2,1)}, u32[]{:S(2)}, u32[]{:S(2)}) collective-permute-start(bf16[2,288,1024]{2,1,0:T(8,128)(2,1)S(1)} %fusion.16), channel_id=1, source_target_pairs={{0,2},{2,0},{4,6},{6,4},{8,10},{10,8},{12,14},{14,12},{16,18},{18,... | collective-permute-start | bytes 3538952 | tf_op jit(solution)/shard_map/ppermute | solution.py:33
  65.6 16.3 %collective-permute-start.9 = (bf16[288,1024]{1,0:T(8,128)(2,1)S(1)}, bf16[288,1024]{1,0:T(8,128)(2,1)S(1)}, u32[]{:S(2)}, u32[]{:S(2)}) collective-permute-start(bf16[288,1024]{1,0:T(8,128)(2,1)S(1)} %fusion.38), channel_id=1, source_target_pairs={{0,4},{2,6},{4,0},{6,2},{8,12},{10,14},{12,8},{14,10},{16,20},{18,... | collective-permute-start | bytes 1769480 | tf_op jit(solution)/shard_map/ppermute | solution.py:33
  70.6 40.5 %collective-permute-start.5 = (bf16[384,2304]{1,0:T(8,128)(2,1)}, bf16[384,2304]{1,0:T(8,128)(2,1)S(1)}, u32[]{:S(2)}, u32[]{:S(2)}) collective-permute-start(bf16[384,2304]{1,0:T(8,128)(2,1)} %fusion.6), channel_id=1, source_target_pairs={{0,1},{1,0},{2,3},{3,2},{4,5},{5,4},{6,7},{7,6},{8,9},{9,8},{10,11... | collective-permute-start | bytes 5308424 | tf_op jit(solution)/shard_map/ppermute | solution.py:23
  74.0 20.4 %collective-permute-start.7 = (bf16[288,1024]{1,0:T(8,128)(2,1)S(1)}, bf16[288,1024]{1,0:T(8,128)(2,1)S(1)}, u32[]{:S(2)}, u32[]{:S(2)}) collective-permute-start(bf16[288,1024]{1,0:T(8,128)(2,1)S(1)} %fusion.37), channel_id=1, source_target_pairs={{0,4},{2,6},{4,0},{6,2},{8,12},{10,14},{12,8},{14,10},{16,20},{18,... | collective-permute-start | bytes 1769480 | tf_op jit(solution)/shard_map/ppermute | solution.py:33
  82.0 13.6 %collective-permute-start.10 = (bf16[288,1024]{1,0:T(8,128)(2,1)S(1)}, bf16[288,1024]{1,0:T(8,128)(2,1)S(1)}, u32[]{:S(2)}, u32[]{:S(2)}) collective-permute-start(bf16[288,1024]{1,0:T(8,128)(2,1)S(1)} %fusion.20), channel_id=1, source_target_pairs={{0,8},{2,10},{4,12},{6,14},{8,0},{10,2},{12,4},{14,6},{16,24},{18,... | collective-permute-start | bytes 1769480 | tf_op jit(solution)/shard_map/ppermute | solution.py:40
  85.8 26.7 %collective-permute-start.15 = (bf16[288,1024]{1,0:T(8,128)(2,1)S(1)}, bf16[288,1024]{1,0:T(8,128)(2,1)S(1)}, u32[]{:S(2)}, u32[]{:S(2)}) collective-permute-start(bf16[288,1024]{1,0:T(8,128)(2,1)S(1)} %fusion.40), channel_id=1, source_target_pairs={{0,4},{2,6},{4,0},{6,2},{8,12},{10,14},{12,8},{14,10},{16,20},{18,... | collective-permute-start | bytes 1769480 | tf_op jit(solution)/shard_map/ppermute | solution.py:33
  89.3 40.4 %collective-permute-start.13 = (bf16[288,1024]{1,0:T(8,128)(2,1)S(1)}, bf16[288,1024]{1,0:T(8,128)(2,1)S(1)}, u32[]{:S(2)}, u32[]{:S(2)}) collective-permute-start(bf16[288,1024]{1,0:T(8,128)(2,1)S(1)} %fusion.39), channel_id=1, source_target_pairs={{0,4},{2,6},{4,0},{6,2},{8,12},{10,14},{12,8},{14,10},{16,20},{18,... | collective-permute-start | bytes 1769480 | tf_op jit(solution)/shard_map/ppermute | solution.py:33
  95.9 38.1 %collective-permute-start.17 = (bf16[288,1024]{1,0:T(8,128)(2,1)S(1)}, bf16[288,1024]{1,0:T(8,128)(2,1)S(1)}, u32[]{:S(2)}, u32[]{:S(2)}) collective-permute-start(bf16[288,1024]{1,0:T(8,128)(2,1)S(1)} %fusion.22), channel_id=1, source_target_pairs={{0,24},{2,26},{4,28},{6,30},{8,16},{10,18},{12,20},{14,22},{16,8},... | collective-permute-start | bytes 1769480 | tf_op jit(solution)/shard_map/ppermute | solution.py:40
  111.0 3.6 %copy-start.4 = (bf16[384,2304]{1,0:T(8,128)(2,1)}, bf16[384,2304]{1,0:T(8,128)(2,1)S(1)}, u32[]{:S(2)}) copy-start(bf16[384,2304]{1,0:T(8,128)(2,1)S(1)} %collective-permute-done.5) | copy-start | bytes 5308420
  111.0 3.6 %collective-permute-start.11 = (f32[384]{0:T(512)S(1)}, f32[384]{0:T(512)S(1)}, u32[]{:S(2)}, u32[]{:S(2)}) collective-permute-start(f32[384]{0:T(512)S(1)} %get-tuple-element.10), channel_id=1, source_target_pairs={{0,1},{1,0},{2,3},{3,2},{4,5},{5,4},{6,7},{7,6},{8,9},{9,8},{10,11... | collective-permute-start | bytes 4616 | tf_op jit(solution)/shard_map/ppermute | solution.py:23
  112.8 21.3 %collective-permute-start.16 = (bf16[288,1024]{1,0:T(8,128)(2,1)S(1)}, bf16[288,1024]{1,0:T(8,128)(2,1)S(1)}, u32[]{:S(2)}, u32[]{:S(2)}) collective-permute-start(bf16[288,1024]{1,0:T(8,128)(2,1)S(1)} %fusion.17), channel_id=1, source_target_pairs={{0,8},{2,10},{4,12},{6,14},{8,0},{10,2},{12,4},{14,6},{16,24},{18,... | collective-permute-start | bytes 1769480 | tf_op jit(solution)/shard_map/ppermute | solution.py:40
  120.6 1.2 collective-permute-start.18
  121.8 3.7 %collective-permute-start.19 = (f32[2304]{0:T(1024)S(1)}, f32[2304]{0:T(1024)S(1)}, u32[]{:S(2)}, u32[]{:S(2)}) collective-permute-start(f32[2304]{0:T(1024)S(1)} %add.234), channel_id=1, source_target_pairs={{0,4},{2,6},{4,0},{6,2},{8,12},{10,14},{12,8},{14,10},{16,20},{18,... | collective-permute-start | bytes 27656 | tf_op jit(solution)/shard_map/ppermute | solution.py:33
  125.5 5.6 %collective-permute-start.20 = (f32[2304]{0:T(1024)S(1)}, f32[2304]{0:T(1024)S(1)}, u32[]{:S(2)}, u32[]{:S(2)}) collective-permute-start(f32[2304]{0:T(1024)S(1)} %add.235), channel_id=1, source_target_pairs={{0,8},{2,10},{4,12},{6,14},{8,16},{10,18},{12,20},{14,22},{16,24},... | collective-permute-start | bytes 27656 | tf_op jit(solution)/shard_map/ppermute | solution.py:33
  127.1 4.6 %collective-permute-start.21 = (f32[2304]{0:T(1024)S(1)}, f32[2304]{0:T(1024)S(1)}, u32[]{:S(2)}, u32[]{:S(2)}) collective-permute-start(f32[2304]{0:T(1024)S(1)} %add.235), channel_id=1, source_target_pairs={{0,16},{2,18},{4,20},{6,22},{8,24},{10,26},{12,28},{14,30},{16,0},... | collective-permute-start | bytes 27656 | tf_op jit(solution)/shard_map/ppermute | solution.py:33
  129.7 3.7 %collective-permute-start.22 = (f32[2304]{0:T(1024)S(1)}, f32[2304]{0:T(1024)S(1)}, u32[]{:S(2)}, u32[]{:S(2)}) collective-permute-start(f32[2304]{0:T(1024)S(1)} %add.235), channel_id=1, source_target_pairs={{0,24},{2,26},{4,28},{6,30},{8,0},{10,2},{12,4},{14,6},{16,8},{18,... | collective-permute-start | bytes 27656 | tf_op jit(solution)/shard_map/ppermute | solution.py:33

commit v3 on v2

--- a/solution.py
+++ b/solution.py
@@ -46,18 +46,18 @@
         d = lax.axis_index("dp")
         a, b, c = d // (nb * nc), (d // nc) % nb, d % nc
 
-        own_sq = jnp.sum(jnp.square(h.astype(f32)), axis=1)
+        nchunk = 3 if rows % 3 == 0 else 1
+        step = rows // nchunk
+        got = [[h[i * step:(i + 1) * step] for i in range(nchunk)]] + [[] for _ in range(1, nt)]
+        lead = lax.optimization_barrier(got[0][0])
+        own_sq = jnp.sum(jnp.square(after(h, lead).astype(f32)), axis=1)
+        for i in range(nchunk):
+            piece = lead if i == 0 else after(got[0][i], own_sq)
+            for k in range(1, nt):
+                got[k].append(shift_tensor(piece, k))
         sq = own_sq
         for k in range(1, nt):
             sq = sq + shift_tensor(own_sq, k)
-        nchunk = 3 if rows % 3 == 0 else 1
-        step = rows // nchunk
-        got = [[] for _ in range(nt)]
-        for i in range(nchunk):
-            piece = h[i * step:(i + 1) * step]
-            got[0].append(piece)
-            for k in range(1, nt):
-                got[k].append(shift_tensor(piece, k))
         scaled = lax.rsqrt(sq / width + epsilon)
 
         def w_block(k):
@@ -102,9 +102,11 @@
 
         block = width // na
         small = width // ndp
+        head_grad = dlogits
+
         def halves(to):
             cut = lax.dynamic_slice_in_dim(normed, to * block, block, axis=1)
-            prod = lax.dot_general(cut, dlogits, (((0,), (0,)), ((), ())),
+            prod = lax.dot_general(cut, head_grad, (((0,), (0,)), ((), ())),
                                    preferred_element_type=f32)
             prod = prod.reshape(nb, nc, small, vocab)
             keep = lax.dynamic_index_in_dim(prod, c, axis=1, keepdims=False)

time: 136 us -> 134 us (0.985)
  starting transfers between devices: 30.9 us -> 28.2 us
    ppermute x7, starting transfers between devices: 12 us -> 9.83 us  [shift_tensor(): return lax.ppermute(x, 'tensor', [(i, (i + k) % nt) for i in range(nt)])]
  transfers between devices with their start and end apart: 23 -> 23, of which waited for: 14 -> 13; matrix products, arithmetic and copies ran while one was open for 17% -> 19% of each run, Pallas kernels for 0% -> 0%
where the time goes in v3:
time: 134 us
  waiting for transfers between devices  69.1 us (52%)
  starting transfers between devices  28.2 us (21%)
  matrix products  19.6 us (15%)
  other arithmetic  13.1 us (10%)
  local copies, waits for them, and re-layouts  2.58 us (2%)
    ppermute x7, waiting for transfers between devices, shift_tensor(): return lax.ppermute(x, 'tensor', [(i, (i + k) % nt) for i in range(nt)])  49 us
    ppermute x13, waiting for transfers between devices, dp_shift(): return lax.ppermute(x, 'dp', pairs)  19 us
    ppermute x13, starting transfers between devices, dp_shift(): return lax.ppermute(x, 'dp', pairs)  11.6 us
    ppermute x7, starting transfers between devices, shift_tensor(): return lax.ppermute(x, 'tensor', [(i, (i + k) % nt) for i in range(nt)])  9.83 us
    ppermute x3, starting transfers between devices, dp_to(): return lax.ppermute(x, 'dp', pairs)  6.78 us
    dot_general x1, matrix products, shards(): lax.dot_general(dlogits, w_block(0), (((1,), (1,)), ((), ())), preferred_...  6.01 us
    add x4, other arithmetic, halves(): keep = keep + dp_shift(away, 0, 0, 1).astype(f32)  5.82 us
    dot_general x4, matrix products, halves(): lax.dot_general(cut, head_grad, (((0,), (0,)), ((), ())), preferred_eleme...  5.76 us
  transfers between devices with their start and end apart: 23, of which 13 were waited for; matrix products, arithmetic and copies ran while one was open for 19% of the time, Pallas kernels for 0%

profile of v3, /device:TPU:0, one launch (start us, length us, event | category | flops | bytes accessed | tf_op | source)
XLA Modules:
  0.0 133.6 jit_solution(17230192494831997502)
XLA Ops:
  1.8 3.0 %collective-permute-start.1 = (bf16[128,2304]{1,0:T(8,128)(2,1)S(1)}, bf16[128,2304]{1,0:T(8,128)(2,1)S(1)}, u32[]{:S(2)}, u32[]{:S(2)}) collective-permute-start(bf16[128,2304]{1,0:T(8,128)(2,1)S(1)} %slice.25), channel_id=1, source_target_pairs={{0,1},{1,0},{2,3},{3,2},{4,5},{5,4},{6,7},{7,6},{8,9},{9,8},{10,11... | collective-permute-start | bytes 1769480 | tf_op jit(solution)/shard_map/ppermute | solution.py:23
  4.8 1.9 %multiply_reduce_fusion.1 = f32[384]{0:T(512)S(1)} fusion(bf16[384,2304]{1,0:T(8,128)(2,1)} %param.4), kind=kLoop, calls=%fused_computation.10 | loop fusion | flops 2653824 | bytes 1771008 | tf_op jit(solution)/shard_map/reduce_sum | solution.py:53
  7.0 11.1 %collective-permute-done = f32[384]{0:T(512)S(1)} collective-permute-done((f32[384]{0:T(512)S(1)}, f32[384]{0:T(512)S(1)}, u32[]{:S(2)}, u32[]{:S(2)}) %collective-permute-start) | collective-permute-done | bytes 1568 | tf_op jit(solution)/shard_map/ppermute | solution.py:23
  18.5 1.8 %collective-permute-start.2 = (bf16[128,2304]{1,0:T(8,128)(2,1)S(1)}, bf16[128,2304]{1,0:T(8,128)(2,1)S(1)}, u32[]{:S(2)}, u32[]{:S(2)}) collective-permute-start(bf16[128,2304]{1,0:T(8,128)(2,1)S(1)} %get-tuple-element.12), channel_id=1, source_target_pairs={{0,1},{1,0},{2,3},{3,2},{4,5},{5,4},{6,7},{7,6},{8,9},{9,8},{10,11... | collective-permute-start | bytes 1769480 | tf_op jit(solution)/shard_map/ppermute | solution.py:23
  21.2 13.6 %collective-permute-done.2 = bf16[128,2304]{1,0:T(8,128)(2,1)S(1)} collective-permute-done((bf16[128,2304]{1,0:T(8,128)(2,1)S(1)}, bf16[128,2304]{1,0:T(8,128)(2,1)S(1)}, u32[]{:S(2)}, u32[]{:S(2)}) %collective-permute-start.2) | collective-permute-done | bytes 589856 | tf_op jit(solution)/shard_map/ppermute | solution.py:23
  34.9 10.9 %collective-permute-done.3 = bf16[128,2304]{1,0:T(8,128)(2,1)S(1)} collective-permute-done((bf16[128,2304]{1,0:T(8,128)(2,1)S(1)}, bf16[128,2304]{1,0:T(8,128)(2,1)S(1)}, u32[]{:S(2)}, u32[]{:S(2)}) %collective-permute-start.3) | collective-permute-done | bytes 589856 | tf_op jit(solution)/shard_map/ppermute | solution.py:23
  46.2 1.5 %fusion.46 = f32[128,1024]{1,0:T(8,128)S(1)} fusion(bf16[128,4608]{1,0:T(8,128)(2,1)S(1)} %get-tuple-element.30, bf16[4608,1024]{1,0:T(8,128)(2,1)S(1)} %copy-done), kind=kOutput, calls=%fused_computation.85 | convolution fusion | flops 1207959552 | bytes 11141120 | tf_op jit(solution)/shard_map/dot_general | solution.py:79
  47.8 1.5 %fusion.47 = f32[128,1024]{1,0:T(8,128)S(1)} fusion(bf16[128,4608]{1,0:T(8,128)(2,1)S(1)} %get-tuple-element.32, bf16[4608,1024]{1,0:T(8,128)(2,1)S(1)} %copy-done), kind=kOutput, calls=%fused_computation.86 | convolution fusion | flops 1207959552 | bytes 11141120 | tf_op jit(solution)/shard_map/dot_general | solution.py:79
  49.3 1.5 %fusion.48 = f32[128,1024]{1,0:T(8,128)S(1)} fusion(bf16[128,4608]{1,0:T(8,128)(2,1)S(1)} %get-tuple-element.31, bf16[4608,1024]{1,0:T(8,128)(2,1)S(1)} %copy-done), kind=kOutput, calls=%fused_computation.87 | convolution fusion | flops 1207959552 | bytes 11141120 | tf_op jit(solution)/shard_map/dot_general | solution.py:79
  51.5 1.5 %collective-permute-start.4 = (f32[2,384]{1,0:T(2,128)S(1)}, f32[2,384]{1,0:T(2,128)S(1)}, u32[]{:S(2)}, u32[]{:S(2)}) collective-permute-start(f32[2,384]{1,0:T(2,128)S(1)} %pad_maximum_fusion.2), channel_id=1, source_target_pairs={{0,1},{1,0},{2,3},{3,2},{4,5},{5,4},{6,7},{7,6},{8,9},{9,8},{10,11... | collective-permute-start | bytes 9224 | tf_op jit(solution)/shard_map/ppermute | solution.py:23
  53.4 1.7 %collective-permute-done.4 = f32[2,384]{1,0:T(2,128)S(1)} collective-permute-done((f32[2,384]{1,0:T(2,128)S(1)}, f32[2,384]{1,0:T(2,128)S(1)}, u32[]{:S(2)}, u32[]{:S(2)}) %collective-permute-start.4) | collective-permute-done | bytes 3104 | tf_op jit(solution)/shard_map/ppermute | solution.py:23
  55.8 1.5 %fusion.21 = f32[1152,1024]{1,0:T(8,128)S(1)} fusion(bf16[384,1024]{1,0:T(8,128)(2,1)S(1)} %get-tuple-element.22, bf16[384,4608]{1,0:T(8,128)(2,1)S(1)} %pad_maximum_fusion, s32[]{:T(128)S(6)} %select_n.133), kind=kOutput, calls=%fused_computation.51 | convolution fusion | flops 905969664 | bytes 6389764 | tf_op jit(solution)/shard_map/dot_general | solution.py:109
  57.5 1.4 %fusion.23 = f32[1152,1024]{1,0:T(8,128)S(1)} fusion(bf16[384,1024]{1,0:T(8,128)(2,1)S(1)} %get-tuple-element.22, bf16[384,4608]{1,0:T(8,128)(2,1)S(1)} %pad_maximum_fusion, s32[]{:T(128)S(6)} %select_n.124), kind=kOutput, calls=%fused_computation.53 | convolution fusion | flops 905969664 | bytes 6389764 | tf_op jit(solution)/shard_map/dot_general | solution.py:109
  64.1 1.5 %collective-permute-start.9 = (bf16[288,1024]{1,0:T(8,128)(2,1)S(1)}, bf16[288,1024]{1,0:T(8,128)(2,1)S(1)}, u32[]{:S(2)}, u32[]{:S(2)}) collective-permute-start(bf16[288,1024]{1,0:T(8,128)(2,1)S(1)} %fusion.32), channel_id=1, source_target_pairs={{0,4},{2,6},{4,0},{6,2},{8,12},{10,14},{12,8},{14,10},{16,20},{18,... | collective-permute-start | bytes 1769480 | tf_op jit(solution)/shard_map/ppermute | solution.py:33
  65.6 3.3 %fusion.4 = bf16[384,2304]{1,0:T(8,128)(2,1)} fusion(bf16[384,1024]{1,0:T(8,128)(2,1)S(1)} %get-tuple-element.22, bf16[4608,1024]{1,0:T(8,128)(2,1)S(1)} %copy-done, s32[]{:T(128)S(6)} %select_n.122), kind=kOutput, calls=%fused_computation.4 | convolution fusion | flops 1812824064 | bytes 7274500 | tf_op jit(solution)/shard_map/dot_general | solution.py:99
  68.8 1.5 %collective-permute-start.5 = (bf16[384,2304]{1,0:T(8,128)(2,1)}, bf16[384,2304]{1,0:T(8,128)(2,1)S(1)}, u32[]{:S(2)}, u32[]{:S(2)}) collective-permute-start(bf16[384,2304]{1,0:T(8,128)(2,1)} %fusion.4), channel_id=1, source_target_pairs={{0,1},{1,0},{2,3},{3,2},{4,5},{5,4},{6,7},{7,6},{8,9},{9,8},{10,11... | collective-permute-start | bytes 5308424 | tf_op jit(solution)/shard_map/ppermute | solution.py:23
  70.4 1.8 %bitcast_add_fusion.3 = f32[2,288,1024]{2,1,0:T(8,128)S(1)} fusion(bf16[2,288,1024]{2,1,0:T(8,128)(2,1)} %collective-permute-done.6, f32[2,2,288,1024]{3,2,1,0:T(8,128)S(1)} %bitcast.81, s32[]{:T(128)S(6)} %select_n.126), kind=kLoop, calls=%fused_computation.18 | loop fusion | flops 1179648 | bytes 5898244 | tf_op jit(solution)/shard_map/add | solution.py:114
  72.9 7.5 %collective-permute-done.9 = bf16[288,1024]{1,0:T(8,128)(2,1)S(1)} collective-permute-done((bf16[288,1024]{1,0:T(8,128)(2,1)S(1)}, bf16[288,1024]{1,0:T(8,128)(2,1)S(1)}, u32[]{:S(2)}, u32[]{:S(2)}) %collective-permute-start.9) | collective-permute-done | bytes 589856 | tf_op jit(solution)/shard_map/ppermute | solution.py:33
  80.6 1.6 %collective-permute-start.10 = (bf16[288,1024]{1,0:T(8,128)(2,1)S(1)}, bf16[288,1024]{1,0:T(8,128)(2,1)S(1)}, u32[]{:S(2)}, u32[]{:S(2)}) collective-permute-start(bf16[288,1024]{1,0:T(8,128)(2,1)S(1)} %fusion.14), channel_id=1, source_target_pairs={{0,8},{2,10},{4,12},{6,14},{8,0},{10,2},{12,4},{14,6},{16,24},{18,... | collective-permute-start | bytes 1769480 | tf_op jit(solution)/shard_map/ppermute | solution.py:40
  82.1 1.8 %bitcast_add_fusion = f32[2,288,1024]{2,1,0:T(8,128)S(1)} fusion(bf16[2,288,1024]{2,1,0:T(8,128)(2,1)} %collective-permute-done.14, f32[2,2,288,1024]{3,2,1,0:T(8,128)S(1)} %bitcast.79, s32[]{:T(128)S(6)} %select_n.126), kind=kLoop, calls=%fused_computation.15 | loop fusion | flops 1179648 | bytes 5898244 | tf_op jit(solution)/shard_map/add | solution.py:114
  84.1 1.5 %collective-permute-start.15 = (bf16[288,1024]{1,0:T(8,128)(2,1)S(1)}, bf16[288,1024]{1,0:T(8,128)(2,1)S(1)}, u32[]{:S(2)}, u32[]{:S(2)}) collective-permute-start(bf16[288,1024]{1,0:T(8,128)(2,1)S(1)} %fusion.34), channel_id=1, source_target_pairs={{0,4},{2,6},{4,0},{6,2},{8,12},{10,14},{12,8},{14,10},{16,20},{18,... | collective-permute-start | bytes 1769480 | tf_op jit(solution)/shard_map/ppermute | solution.py:33
  85.6 1.8 %bitcast_add_fusion.1 = f32[2,288,1024]{2,1,0:T(8,128)S(1)} fusion(bf16[2,288,1024]{2,1,0:T(8,128)(2,1)} %collective-permute-done.12, f32[2,2,288,1024]{3,2,1,0:T(8,128)S(1)} %bitcast.77, s32[]{:T(128)S(6)} %select_n.126), kind=kLoop, calls=%fused_computation.16 | loop fusion | flops 1179648 | bytes 5898244 | tf_op jit(solution)/shard_map/add | solution.py:114
  88.1 4.9 %collective-permute-done.7 = bf16[288,1024]{1,0:T(8,128)(2,1)S(1)} collective-permute-done((bf16[288,1024]{1,0:T(8,128)(2,1)S(1)}, bf16[288,1024]{1,0:T(8,128)(2,1)S(1)}, u32[]{:S(2)}, u32[]{:S(2)}) %collective-permute-start.7) | collective-permute-done | bytes 589856 | tf_op jit(solution)/shard_map/ppermute | solution.py:33
  94.4 3.6 %collective-permute-start.17 = (bf16[288,1024]{1,0:T(8,128)(2,1)S(1)}, bf16[288,1024]{1,0:T(8,128)(2,1)S(1)}, u32[]{:S(2)}, u32[]{:S(2)}) collective-permute-start(bf16[288,1024]{1,0:T(8,128)(2,1)S(1)} %fusion.16), channel_id=1, source_target_pairs={{0,24},{2,26},{4,28},{6,30},{8,16},{10,18},{12,20},{14,22},{16,8},... | collective-permute-start | bytes 1769480 | tf_op jit(solution)/shard_map/ppermute | solution.py:40
  98.0 11.3 %collective-permute-done.5 = bf16[384,2304]{1,0:T(8,128)(2,1)S(1)} collective-permute-done((bf16[384,2304]{1,0:T(8,128)(2,1)}, bf16[384,2304]{1,0:T(8,128)(2,1)S(1)}, u32[]{:S(2)}, u32[]{:S(2)}) %collective-permute-start.5) | collective-permute-done | bytes 1769504 | tf_op jit(solution)/shard_map/ppermute | solution.py:23
  109.3 1.5 %collective-permute-start.11 = (f32[384]{0:T(512)S(1)}, f32[384]{0:T(512)S(1)}, u32[]{:S(2)}, u32[]{:S(2)}) collective-permute-start(f32[384]{0:T(512)S(1)} %get-tuple-element.16), channel_id=1, source_target_pairs={{0,1},{1,0},{2,3},{3,2},{4,5},{5,4},{6,7},{7,6},{8,9},{9,8},{10,11... | collective-permute-start | bytes 4616 | tf_op jit(solution)/shard_map/ppermute | solution.py:23
  111.0 1.6 %collective-permute-start.16 = (bf16[288,1024]{1,0:T(8,128)(2,1)S(1)}, bf16[288,1024]{1,0:T(8,128)(2,1)S(1)}, u32[]{:S(2)}, u32[]{:S(2)}) collective-permute-start(bf16[288,1024]{1,0:T(8,128)(2,1)S(1)} %fusion.11), channel_id=1, source_target_pairs={{0,8},{2,10},{4,12},{6,14},{8,0},{10,2},{12,4},{14,6},{16,24},{18,... | collective-permute-start | bytes 1769480 | tf_op jit(solution)/shard_map/ppermute | solution.py:40
  112.9 6.0 %multiply_reduce_fusion = (f32[2304]{0:T(1024)S(1)}, f32[384,2304]{1,0:T(8,128)}) fusion(bf16[384,2304]{1,0:T(8,128)(2,1)S(1)} %copy-done.1, bf16[384,2304]{1,0:T(8,128)(2,1)} %copy-done.4, f32[384]{0:T(512)S(1)} %add_rsqrt_fusion, f32[384]{0:T(512)S(1)} %add_multiply_fusion, f32[2304]{0:T(1024)S(1)} %get-tuple-element.29, ...), kind=kOutput, calls=%fused_computation.6 | convolution fusion | flops 1820784384 | bytes 12608516 | tf_op jit(solution)/shard_map/dot_general | solution.py:154
  120.7 3.1 %collective-permute-done.19 = f32[2304]{0:T(1024)S(1)} collective-permute-done((f32[2304]{0:T(1024)S(1)}, f32[2304]{0:T(1024)S(1)}, u32[]{:S(2)}, u32[]{:S(2)}) %collective-permute-start.19) | collective-permute-done | bytes 9248 | tf_op jit(solution)/shard_map/ppermute | solution.py:33
  123.8 1.6 %collective-permute-start.20 = (f32[2304]{0:T(1024)S(1)}, f32[2304]{0:T(1024)S(1)}, u32[]{:S(2)}, u32[]{:S(2)}) collective-permute-start(f32[2304]{0:T(1024)S(1)} %add.235), channel_id=1, source_target_pairs={{0,8},{2,10},{4,12},{6,14},{8,16},{10,18},{12,20},{14,22},{16,24},... | collective-permute-start | bytes 27656 | tf_op jit(solution)/shard_map/ppermute | solution.py:33
  125.4 2.6 %collective-permute-start.21 = (f32[2304]{0:T(1024)S(1)}, f32[2304]{0:T(1024)S(1)}, u32[]{:S(2)}, u32[]{:S(2)}) collective-permute-start(f32[2304]{0:T(1024)S(1)} %add.235), channel_id=1, source_target_pairs={{0,16},{2,18},{4,20},{6,22},{8,24},{10,26},{12,28},{14,30},{16,0},... | collective-permute-start | bytes 27656 | tf_op jit(solution)/shard_map/ppermute | solution.py:33
  130.0 1.7 %collective-permute-done.22 = f32[2304]{0:T(1024)S(1)} collective-permute-done((f32[2304]{0:T(1024)S(1)}, f32[2304]{0:T(1024)S(1)}, u32[]{:S(2)}, u32[]{:S(2)}) %collective-permute-start.22) | collective-permute-done | bytes 9248 | tf_op jit(solution)/shard_map/ppermute | solution.py:33
  (75 shorter events, 19.3 us)
Async XLA Ops:
  0.6 6.3 %copy-start.2 = (f32[4608]{0:T(1024)S(1)}, f32[4608]{0:T(1024)}, u32[]{:S(2)}) copy-start(f32[4608]{0:T(1024)} %param.5) | copy-start | bytes 55300
  1.8 16.5 %copy-start.1 = (bf16[384,2304]{1,0:T(8,128)(2,1)S(1)}, bf16[384,2304]{1,0:T(8,128)(2,1)}, u32[]{:S(2)}) copy-start(bf16[384,2304]{1,0:T(8,128)(2,1)} %param.4) | copy-start | bytes 5308420
  1.8 19.4 %collective-permute-start.1 = (bf16[128,2304]{1,0:T(8,128)(2,1)S(1)}, bf16[128,2304]{1,0:T(8,128)(2,1)S(1)}, u32[]{:S(2)}, u32[]{:S(2)}) collective-permute-start(bf16[128,2304]{1,0:T(8,128)(2,1)S(1)} %slice.25), channel_id=1, source_target_pairs={{0,1},{1,0},{2,3},{3,2},{4,5},{5,4},{6,7},{7,6},{8,9},{9,8},{10,11... | collective-permute-start | bytes 1769480 | tf_op jit(solution)/shard_map/ppermute | solution.py:23
  6.7 11.5 %collective-permute-start = (f32[384]{0:T(512)S(1)}, f32[384]{0:T(512)S(1)}, u32[]{:S(2)}, u32[]{:S(2)}) collective-permute-start(f32[384]{0:T(512)S(1)} %multiply_reduce_fusion.1), channel_id=1, source_target_pairs={{0,1},{1,0},{2,3},{3,2},{4,5},{5,4},{6,7},{7,6},{8,9},{9,8},{10,11... | collective-permute-start | bytes 4616 | tf_op jit(solution)/shard_map/ppermute | solution.py:23
  18.3 27.9 %copy-start = (bf16[4608,1024]{1,0:T(8,128)(2,1)S(1)}, bf16[4608,1024]{1,0:T(8,128)(2,1)}, u32[]{:S(2)}) copy-start(bf16[4608,1024]{1,0:T(8,128)(2,1)} %param.6) | copy-start | bytes 28311556
  18.5 16.3 %collective-permute-start.2 = (bf16[128,2304]{1,0:T(8,128)(2,1)S(1)}, bf16[128,2304]{1,0:T(8,128)(2,1)S(1)}, u32[]{:S(2)}, u32[]{:S(2)}) collective-permute-start(bf16[128,2304]{1,0:T(8,128)(2,1)S(1)} %get-tuple-element.12), channel_id=1, source_target_pairs={{0,1},{1,0},{2,3},{3,2},{4,5},{5,4},{6,7},{7,6},{8,9},{9,8},{10,11... | collective-permute-start | bytes 1769480 | tf_op jit(solution)/shard_map/ppermute | solution.py:23
  20.3 25.4 %collective-permute-start.3 = (bf16[128,2304]{1,0:T(8,128)(2,1)S(1)}, bf16[128,2304]{1,0:T(8,128)(2,1)S(1)}, u32[]{:S(2)}, u32[]{:S(2)}) collective-permute-start(bf16[128,2304]{1,0:T(8,128)(2,1)S(1)} %get-tuple-element.13), channel_id=1, source_target_pairs={{0,1},{1,0},{2,3},{3,2},{4,5},{5,4},{6,7},{7,6},{8,9},{9,8},{10,11... | collective-permute-start | bytes 1769480 | tf_op jit(solution)/shard_map/ppermute | solution.py:23
  51.5 3.7 %copy-start.3 = (s32[384]{0:T(512)S(1)}, s32[384]{0:T(512)}, u32[]{:S(2)}) copy-start(s32[384]{0:T(512)} %param.7) | copy-start | bytes 4612
  51.5 3.7 %collective-permute-start.4 = (f32[2,384]{1,0:T(2,128)S(1)}, f32[2,384]{1,0:T(2,128)S(1)}, u32[]{:S(2)}, u32[]{:S(2)}) collective-permute-start(f32[2,384]{1,0:T(2,128)S(1)} %pad_maximum_fusion.2), channel_id=1, source_target_pairs={{0,1},{1,0},{2,3},{3,2},{4,5},{5,4},{6,7},{7,6},{8,9},{9,8},{10,11... | collective-permute-start | bytes 9224 | tf_op jit(solution)/shard_map/ppermute | solution.py:23
  57.5 6.2 %collective-permute-start.8 = (bf16[2,288,1024]{2,1,0:T(8,128)(2,1)S(1)}, bf16[2,288,1024]{2,1,0:T(8,128)(2,1)S(1)}, u32[]{:S(2)}, u32[]{:S(2)}) collective-permute-start(bf16[2,288,1024]{2,1,0:T(8,128)(2,1)S(1)} %fusion.8), channel_id=1, source_target_pairs={{0,2},{2,0},{4,6},{6,4},{8,10},{10,8},{12,14},{14,12},{16,18},{18,... | collective-permute-start | bytes 3538952 | tf_op jit(solution)/shard_map/ppermute | solution.py:33
  59.2 11.2 %collective-permute-start.6 = (bf16[2,288,1024]{2,1,0:T(8,128)(2,1)S(1)}, bf16[2,288,1024]{2,1,0:T(8,128)(2,1)}, u32[]{:S(2)}, u32[]{:S(2)}) collective-permute-start(bf16[2,288,1024]{2,1,0:T(8,128)(2,1)S(1)} %fusion.7), channel_id=1, source_target_pairs={{0,2},{2,0},{4,6},{6,4},{8,10},{10,8},{12,14},{14,12},{16,18},{18,... | collective-permute-start | bytes 3538952 | tf_op jit(solution)/shard_map/ppermute | solution.py:33
  61.4 24.3 %collective-permute-start.12 = (bf16[2,288,1024]{2,1,0:T(8,128)(2,1)S(1)}, bf16[2,288,1024]{2,1,0:T(8,128)(2,1)}, u32[]{:S(2)}, u32[]{:S(2)}) collective-permute-start(bf16[2,288,1024]{2,1,0:T(8,128)(2,1)S(1)} %fusion.9), channel_id=1, source_target_pairs={{0,2},{2,0},{4,6},{6,4},{8,10},{10,8},{12,14},{14,12},{16,18},{18,... | collective-permute-start | bytes 3538952 | tf_op jit(solution)/shard_map/ppermute | solution.py:33
  63.1 19.1 %collective-permute-start.14 = (bf16[2,288,1024]{2,1,0:T(8,128)(2,1)S(1)}, bf16[2,288,1024]{2,1,0:T(8,128)(2,1)}, u32[]{:S(2)}, u32[]{:S(2)}) collective-permute-start(bf16[2,288,1024]{2,1,0:T(8,128)(2,1)S(1)} %fusion.10), channel_id=1, source_target_pairs={{0,2},{2,0},{4,6},{6,4},{8,10},{10,8},{12,14},{14,12},{16,18},{18,... | collective-permute-start | bytes 3538952 | tf_op jit(solution)/shard_map/ppermute | solution.py:33
  64.1 16.3 %collective-permute-start.9 = (bf16[288,1024]{1,0:T(8,128)(2,1)S(1)}, bf16[288,1024]{1,0:T(8,128)(2,1)S(1)}, u32[]{:S(2)}, u32[]{:S(2)}) collective-permute-start(bf16[288,1024]{1,0:T(8,128)(2,1)S(1)} %fusion.32), channel_id=1, source_target_pairs={{0,4},{2,6},{4,0},{6,2},{8,12},{10,14},{12,8},{14,10},{16,20},{18,... | collective-permute-start | bytes 1769480 | tf_op jit(solution)/shard_map/ppermute | solution.py:33
  68.8 40.5 %collective-permute-start.5 = (bf16[384,2304]{1,0:T(8,128)(2,1)}, bf16[384,2304]{1,0:T(8,128)(2,1)S(1)}, u32[]{:S(2)}, u32[]{:S(2)}) collective-permute-start(bf16[384,2304]{1,0:T(8,128)(2,1)} %fusion.4), channel_id=1, source_target_pairs={{0,1},{1,0},{2,3},{3,2},{4,5},{5,4},{6,7},{7,6},{8,9},{9,8},{10,11... | collective-permute-start | bytes 5308424 | tf_op jit(solution)/shard_map/ppermute | solution.py:23
  72.3 20.7 %collective-permute-start.7 = (bf16[288,1024]{1,0:T(8,128)(2,1)S(1)}, bf16[288,1024]{1,0:T(8,128)(2,1)S(1)}, u32[]{:S(2)}, u32[]{:S(2)}) collective-permute-start(bf16[288,1024]{1,0:T(8,128)(2,1)S(1)} %fusion.31), channel_id=1, source_target_pairs={{0,4},{2,6},{4,0},{6,2},{8,12},{10,14},{12,8},{14,10},{16,20},{18,... | collective-permute-start | bytes 1769480 | tf_op jit(solution)/shard_map/ppermute | solution.py:33
  80.6 13.5 %collective-permute-start.10 = (bf16[288,1024]{1,0:T(8,128)(2,1)S(1)}, bf16[288,1024]{1,0:T(8,128)(2,1)S(1)}, u32[]{:S(2)}, u32[]{:S(2)}) collective-permute-start(bf16[288,1024]{1,0:T(8,128)(2,1)S(1)} %fusion.14), channel_id=1, source_target_pairs={{0,8},{2,10},{4,12},{6,14},{8,0},{10,2},{12,4},{14,6},{16,24},{18,... | collective-permute-start | bytes 1769480 | tf_op jit(solution)/shard_map/ppermute | solution.py:40
  84.1 26.8 %collective-permute-start.15 = (bf16[288,1024]{1,0:T(8,128)(2,1)S(1)}, bf16[288,1024]{1,0:T(8,128)(2,1)S(1)}, u32[]{:S(2)}, u32[]{:S(2)}) collective-permute-start(bf16[288,1024]{1,0:T(8,128)(2,1)S(1)} %fusion.34), channel_id=1, source_target_pairs={{0,4},{2,6},{4,0},{6,2},{8,12},{10,14},{12,8},{14,10},{16,20},{18,... | collective-permute-start | bytes 1769480 | tf_op jit(solution)/shard_map/ppermute | solution.py:33
  87.5 40.4 %collective-permute-start.13 = (bf16[288,1024]{1,0:T(8,128)(2,1)S(1)}, bf16[288,1024]{1,0:T(8,128)(2,1)S(1)}, u32[]{:S(2)}, u32[]{:S(2)}) collective-permute-start(bf16[288,1024]{1,0:T(8,128)(2,1)S(1)} %fusion.33), channel_id=1, source_target_pairs={{0,4},{2,6},{4,0},{6,2},{8,12},{10,14},{12,8},{14,10},{16,20},{18,... | collective-permute-start | bytes 1769480 | tf_op jit(solution)/shard_map/ppermute | solution.py:33
  94.4 37.9 %collective-permute-start.17 = (bf16[288,1024]{1,0:T(8,128)(2,1)S(1)}, bf16[288,1024]{1,0:T(8,128)(2,1)S(1)}, u32[]{:S(2)}, u32[]{:S(2)}) collective-permute-start(bf16[288,1024]{1,0:T(8,128)(2,1)S(1)} %fusion.16), channel_id=1, source_target_pairs={{0,24},{2,26},{4,28},{6,30},{8,16},{10,18},{12,20},{14,22},{16,8},... | collective-permute-start | bytes 1769480 | tf_op jit(solution)/shard_map/ppermute | solution.py:40
  109.3 3.6 %copy-start.4 = (bf16[384,2304]{1,0:T(8,128)(2,1)}, bf16[384,2304]{1,0:T(8,128)(2,1)S(1)}, u32[]{:S(2)}) copy-start(bf16[384,2304]{1,0:T(8,128)(2,1)S(1)} %collective-permute-done.5) | copy-start | bytes 5308420
  109.3 3.6 %collective-permute-start.11 = (f32[384]{0:T(512)S(1)}, f32[384]{0:T(512)S(1)}, u32[]{:S(2)}, u32[]{:S(2)}) collective-permute-start(f32[384]{0:T(512)S(1)} %get-tuple-element.16), channel_id=1, source_target_pairs={{0,1},{1,0},{2,3},{3,2},{4,5},{5,4},{6,7},{7,6},{8,9},{9,8},{10,11... | collective-permute-start | bytes 4616 | tf_op jit(solution)/shard_map/ppermute | solution.py:23
  111.0 21.2 %collective-permute-start.16 = (bf16[288,1024]{1,0:T(8,128)(2,1)S(1)}, bf16[288,1024]{1,0:T(8,128)(2,1)S(1)}, u32[]{:S(2)}, u32[]{:S(2)}) collective-permute-start(bf16[288,1024]{1,0:T(8,128)(2,1)S(1)} %fusion.11), channel_id=1, source_target_pairs={{0,8},{2,10},{4,12},{6,14},{8,0},{10,2},{12,4},{14,6},{16,24},{18,... | collective-permute-start | bytes 1769480 | tf_op jit(solution)/shard_map/ppermute | solution.py:40
  118.9 1.2 collective-permute-start.18
  120.1 3.7 %collective-permute-start.19 = (f32[2304]{0:T(1024)S(1)}, f32[2304]{0:T(1024)S(1)}, u32[]{:S(2)}, u32[]{:S(2)}) collective-permute-start(f32[2304]{0:T(1024)S(1)} %add.234), channel_id=1, source_target_pairs={{0,4},{2,6},{4,0},{6,2},{8,12},{10,14},{12,8},{14,10},{16,20},{18,... | collective-permute-start | bytes 27656 | tf_op jit(solution)/shard_map/ppermute | solution.py:33
  123.8 5.5 %collective-permute-start.20 = (f32[2304]{0:T(1024)S(1)}, f32[2304]{0:T(1024)S(1)}, u32[]{:S(2)}, u32[]{:S(2)}) collective-permute-start(f32[2304]{0:T(1024)S(1)} %add.235), channel_id=1, source_target_pairs={{0,8},{2,10},{4,12},{6,14},{8,16},{10,18},{12,20},{14,22},{16,24},... | collective-permute-start | bytes 27656 | tf_op jit(solution)/shard_map/ppermute | solution.py:33
  125.4 4.6 %collective-permute-start.21 = (f32[2304]{0:T(1024)S(1)}, f32[2304]{0:T(1024)S(1)}, u32[]{:S(2)}, u32[]{:S(2)}) collective-permute-start(f32[2304]{0:T(1024)S(1)} %add.235), channel_id=1, source_target_pairs={{0,16},{2,18},{4,20},{6,22},{8,24},{10,26},{12,28},{14,30},{16,0},... | collective-permute-start | bytes 27656 | tf_op jit(solution)/shard_map/ppermute | solution.py:33
  128.0 3.7 %collective-permute-start.22 = (f32[2304]{0:T(1024)S(1)}, f32[2304]{0:T(1024)S(1)}, u32[]{:S(2)}, u32[]{:S(2)}) collective-permute-start(f32[2304]{0:T(1024)S(1)} %add.235), channel_id=1, source_target_pairs={{0,24},{2,26},{4,28},{6,30},{8,0},{10,2},{12,4},{14,6},{16,8},{18,... | collective-permute-start | bytes 27656 | tf_op jit(solution)/shard_map/ppermute | solution.py:33

commit v4 on v3

--- a/solution.py
+++ b/solution.py
@@ -49,16 +49,10 @@
         nchunk = 3 if rows % 3 == 0 else 1
         step = rows // nchunk
         got = [[h[i * step:(i + 1) * step] for i in range(nchunk)]] + [[] for _ in range(1, nt)]
-        lead = lax.optimization_barrier(got[0][0])
-        own_sq = jnp.sum(jnp.square(after(h, lead).astype(f32)), axis=1)
-        for i in range(nchunk):
-            piece = lead if i == 0 else after(got[0][i], own_sq)
+        pieces = lax.optimization_barrier(got[0])
+        for piece in pieces:
             for k in range(1, nt):
                 got[k].append(shift_tensor(piece, k))
-        sq = own_sq
-        for k in range(1, nt):
-            sq = sq + shift_tensor(own_sq, k)
-        scaled = lax.rsqrt(sq / width + epsilon)
 
         def w_block(k):
             return lax.dynamic_slice_in_dim(head, ((t + k) % nt) * cols, cols, axis=0)
@@ -68,15 +62,22 @@
 
         logit_parts = []
         normed_parts = []
+        scaled_parts = []
         for i in range(nchunk):
-            s = scaled[i * step:(i + 1) * step, None]
+            parts = [got[k][i] for k in range(nt)]
+            if i:
+                parts = [parts[0]] + [after(p, logit_parts[-1]) for p in parts[1:]]
+            sq = sum(jnp.sum(jnp.square(p.astype(f32)), axis=1) for p in parts)
+            scaled = lax.rsqrt(sq / width + epsilon)
             full = jnp.zeros((step, width), bf16)
             for k in range(nt):
                 g = gain_block(-k)[None, :]
-                n = (got[k][i].astype(f32) * s * g).astype(bf16)
+                n = (parts[k].astype(f32) * scaled[:, None] * g).astype(bf16)
                 full = lax.dynamic_update_slice_in_dim(full, n, ((t - k) % nt) * cols, axis=1)
             normed_parts.append(full)
+            scaled_parts.append(scaled)
             logit_parts.append(jnp.dot(full, head, preferred_element_type=f32))
+        scaled = jnp.concatenate(scaled_parts)
         normed = jnp.concatenate(normed_parts, axis=0)
         logits = jnp.concatenate(logit_parts, axis=0)
 
@@ -151,13 +152,16 @@
             dot_all = dot_all + shift_tensor(dot_own, k)
         row_dot = dot_all / width
 
-        grad = lax.dot_general(dlogits, w_block(0), (((1,), (1,)), ((), ())),
-                               preferred_element_type=f32)
-        for p in arrived:
-            grad = grad + p.astype(f32)
+        own = lax.dot_general(dlogits, w_block(0), (((1,), (1,)), ((), ())),
+                              preferred_element_type=f32)
         normalized = h.astype(f32) * scaled[:, None]
+
+        def total_grad(terms):
+            return sum(p.astype(f32) for p in terms)
+
+        gain_grad = jnp.sum(total_grad([own] + arrived) * normalized, axis=0)
+        grad = total_grad(after([own] + arrived, gain_grad))
         hidden = scaled[:, None] * (grad * gain_block(0)[None, :] - normalized * row_dot[:, None])
-        gain_grad = jnp.sum(grad * normalized, axis=0)
         gain_grad = gain_grad + dp_shift(gain_grad, 0, 0, 1)
         gain_grad = gain_grad + dp_shift(gain_grad, 0, 1, 0)
         gain_grad = gain_grad + sum(dp_shift(gain_grad, k, 0, 0) for k in range(1, na))

time: 134 us -> 136 us (1.015)
  waiting for transfers between devices: 69.1 us -> 62.8 us
  local copies, waits for them, and re-layouts: 2.58 us -> 8.11 us
  other arithmetic: 13.1 us -> 15.4 us
    ppermute x7 -> x6, waiting for transfers between devices: 49 us -> 41.2 us  [shift_tensor(): return lax.ppermute(x, 'tensor', [(i, (i + k) % nt) for i in range(nt)])]
    dot_general x3, matrix products: 4.62 us -> 8.14 us  [shards(): logit_parts.append(jnp.dot(full, head, preferred_element_type=f32))]
    dot_general x1, matrix products: 6.01 us -> 2.54 us  [shards(): lax.dot_general(dlogits, w_block(0), (((1,), (1,)), ((), ())), preferred_...]
    convert_element_type x4, local copies, waits for them, and re-layouts: 0.73 us -> 3.8 us  [halves(): lax.dynamic_index_in_dim(prod, 1 - c, axis=1, keepdims=False).astype(bf16)]
    mul x0 -> x1, other arithmetic: none -> 2.89 us  [shards(): scaled[:, None]]
    slice x1, local copies, waits for them, and re-layouts: 1.11 us -> 2.79 us  [shards(): h[i * step:(i + 1) * step]]
    ppermute x13, waiting for transfers between devices: 19 us -> 20.4 us  [dp_shift(): return lax.ppermute(x, 'dp', pairs)]
    ppermute x7 -> x6, starting transfers between devices: 9.83 us -> 9.89 us  [shift_tensor(): return lax.ppermute(x, 'tensor', [(i, (i + k) % nt) for i in range(nt)])]
  transfers between devices with their start and end apart: 23 -> 22, of which waited for: 13 -> 10; matrix products, arithmetic and copies ran while one was open for 19% -> 24% of each run, Pallas kernels for 0% -> 0%
where the time goes in v4:
time: 136 us; the launch traced here: 135 us
  waiting for transfers between devices  62.8 us (46%)
  starting transfers between devices  29.5 us (22%)
  matrix products  18.5 us (14%)
  other arithmetic  15.4 us (11%)
  local copies, waits for them, and re-layouts  8.11 us (6%)
    ppermute x6, waiting for transfers between devices, shift_tensor(): return lax.ppermute(x, 'tensor', [(i, (i + k) % nt) for i in range(nt)])  41.2 us
    ppermute x13, waiting for transfers between devices, dp_shift(): return lax.ppermute(x, 'dp', pairs)  20.4 us
    ppermute x13, starting transfers between devices, dp_shift(): return lax.ppermute(x, 'dp', pairs)  12.2 us
    ppermute x6, starting transfers between devices, shift_tensor(): return lax.ppermute(x, 'tensor', [(i, (i + k) % nt) for i in range(nt)])  9.89 us
    dot_general x3, matrix products, shards(): logit_parts.append(jnp.dot(full, head, preferred_element_type=f32))  8.14 us
    ppermute x3, starting transfers between devices, dp_to(): return lax.ppermute(x, 'dp', pairs)  7.37 us
    add x4, other arithmetic, halves(): keep = keep + dp_shift(away, 0, 0, 1).astype(f32)  5.82 us
    dot_general x4, matrix products, halves(): lax.dot_general(cut, head_grad, (((0,), (0,)), ((), ())), preferred_eleme...  5.76 us
  transfers between devices with their start and end apart: 22, of which 10 were waited for; matrix products, arithmetic and copies ran while one was open for 24% of the time, Pallas kernels for 0%

profile of v4, /device:TPU:0, one launch (start us, length us, event | category | flops | bytes accessed | tf_op | source)
XLA Modules:
  0.0 135.2 jit_solution(5397070745616805486)
XLA Ops:
  0.6 2.8 %fusion.62 = (bf16[128,2304]{1,0:T(8,128)(2,1)}, bf16[128,2304]{1,0:T(8,128)(2,1)}, bf16[128,2304]{1,0:T(8,128)(2,1)}) fusion(bf16[384,2304]{1,0:T(8,128)(2,1)} %param.4), kind=kLoop, calls=%fused_computation.108 | loop fusion | bytes 3538944 | tf_op jit(solution)/shard_map/slice | solution.py:51
  3.4 3.0 %collective-permute-start = (bf16[128,2304]{1,0:T(8,128)(2,1)}, bf16[128,2304]{1,0:T(8,128)(2,1)S(1)}, u32[]{:S(2)}, u32[]{:S(2)}) collective-permute-start(bf16[128,2304]{1,0:T(8,128)(2,1)} %get-tuple-element.15), channel_id=1, source_target_pairs={{0,1},{1,0},{2,3},{3,2},{4,5},{5,4},{6,7},{7,6},{8,9},{9,8},{10,11... | collective-permute-start | bytes 1769480 | tf_op jit(solution)/shard_map/ppermute | solution.py:23
  6.4 2.0 %collective-permute-start.1 = (bf16[128,2304]{1,0:T(8,128)(2,1)}, bf16[128,2304]{1,0:T(8,128)(2,1)S(1)}, u32[]{:S(2)}, u32[]{:S(2)}) collective-permute-start(bf16[128,2304]{1,0:T(8,128)(2,1)} %get-tuple-element.16), channel_id=1, source_target_pairs={{0,1},{1,0},{2,3},{3,2},{4,5},{5,4},{6,7},{7,6},{8,9},{9,8},{10,11... | collective-permute-start | bytes 1769480 | tf_op jit(solution)/shard_map/ppermute | solution.py:23
  9.7 11.0 %collective-permute-done = bf16[128,2304]{1,0:T(8,128)(2,1)S(1)} collective-permute-done((bf16[128,2304]{1,0:T(8,128)(2,1)}, bf16[128,2304]{1,0:T(8,128)(2,1)S(1)}, u32[]{:S(2)}, u32[]{:S(2)}) %collective-permute-start) | collective-permute-done | bytes 589856 | tf_op jit(solution)/shard_map/ppermute | solution.py:23
  21.5 5.4 %fusion.64 = f32[128,1024]{1,0:T(8,128)S(1)} fusion(bf16[128,4608]{1,0:T(8,128)(2,1)S(1)} %fusion.51, bf16[4608,1024]{1,0:T(8,128)(2,1)} %param.6), kind=kOutput, calls=%fused_computation.110 | convolution fusion | flops 1207959552 | bytes 11141120 | tf_op jit(solution)/shard_map/dot_general | solution.py:79
  26.9 18.3 %collective-permute-done.1 = bf16[128,2304]{1,0:T(8,128)(2,1)S(1)} collective-permute-done((bf16[128,2304]{1,0:T(8,128)(2,1)}, bf16[128,2304]{1,0:T(8,128)(2,1)S(1)}, u32[]{:S(2)}, u32[]{:S(2)}) %collective-permute-start.1) | collective-permute-done | bytes 589856 | tf_op jit(solution)/shard_map/ppermute | solution.py:23
  50.6 1.8 %collective-permute-start.3 = (f32[2,384]{1,0:T(2,128)S(1)}, f32[2,384]{1,0:T(2,128)S(1)}, u32[]{:S(2)}, u32[]{:S(2)}) collective-permute-start(f32[2,384]{1,0:T(2,128)S(1)} %pad_maximum_fusion.2), channel_id=1, source_target_pairs={{0,1},{1,0},{2,3},{3,2},{4,5},{5,4},{6,7},{7,6},{8,9},{9,8},{10,11... | collective-permute-start | bytes 9224 | tf_op jit(solution)/shard_map/ppermute | solution.py:23
  52.4 1.8 %collective-permute-done.3 = f32[2,384]{1,0:T(2,128)S(1)} collective-permute-done((f32[2,384]{1,0:T(2,128)S(1)}, f32[2,384]{1,0:T(2,128)S(1)}, u32[]{:S(2)}, u32[]{:S(2)}) %collective-permute-start.3) | collective-permute-done | bytes 3104 | tf_op jit(solution)/shard_map/ppermute | solution.py:23
  56.6 1.4 %fusion.41 = f32[1152,1024]{1,0:T(8,128)S(1)} fusion(bf16[384,1024]{1,0:T(8,128)(2,1)S(1)} %get-tuple-element.33, bf16[384,4608]{1,0:T(8,128)(2,1)S(1)} %pad_maximum_fusion, s32[]{:T(128)S(6)} %select_n.124), kind=kOutput, calls=%fused_computation.75 | convolution fusion | flops 905969664 | bytes 6389764 | tf_op jit(solution)/shard_map/dot_general | solution.py:110
  59.8 1.4 %fusion.35 = f32[1152,1024]{1,0:T(8,128)S(1)} fusion(bf16[384,1024]{1,0:T(8,128)(2,1)S(1)} %get-tuple-element.33, bf16[384,4608]{1,0:T(8,128)(2,1)S(1)} %pad_maximum_fusion, s32[]{:T(128)S(6)} %select_n.135), kind=kOutput, calls=%fused_computation.69 | convolution fusion | flops 905969664 | bytes 6389764 | tf_op jit(solution)/shard_map/dot_general | solution.py:110
  62.4 1.4 %fusion.37 = f32[1152,1024]{1,0:T(8,128)S(1)} fusion(bf16[384,1024]{1,0:T(8,128)(2,1)S(1)} %get-tuple-element.33, bf16[384,4608]{1,0:T(8,128)(2,1)S(1)} %pad_maximum_fusion, s32[]{:T(128)S(6)} %select_n.134), kind=kOutput, calls=%fused_computation.71 | convolution fusion | flops 905969664 | bytes 6389764 | tf_op jit(solution)/shard_map/dot_general | solution.py:110
  66.2 1.8 %collective-permute-start.8 = (bf16[288,1024]{1,0:T(8,128)(2,1)S(1)}, bf16[288,1024]{1,0:T(8,128)(2,1)S(1)}, u32[]{:S(2)}, u32[]{:S(2)}) collective-permute-start(bf16[288,1024]{1,0:T(8,128)(2,1)S(1)} %fusion.44), channel_id=1, source_target_pairs={{0,4},{2,6},{4,0},{6,2},{8,12},{10,14},{12,8},{14,10},{16,20},{18,... | collective-permute-start | bytes 1769480 | tf_op jit(solution)/shard_map/ppermute | solution.py:33
  68.0 2.1 %fusion.4 = bf16[384,2304]{1,0:T(8,128)(2,1)S(1)} fusion(bf16[384,1024]{1,0:T(8,128)(2,1)S(1)} %get-tuple-element.33, bf16[4608,1024]{1,0:T(8,128)(2,1)S(1)} %bitcast.77, s32[]{:T(128)S(6)} %select_n.122), kind=kOutput, calls=%fused_computation.4 | convolution fusion | flops 1812824064 | bytes 7274500 | tf_op jit(solution)/shard_map/dot_general | solution.py:100
  70.1 1.6 %collective-permute-start.4 = (bf16[384,2304]{1,0:T(8,128)(2,1)S(1)}, bf16[384,2304]{1,0:T(8,128)(2,1)S(1)}, u32[]{:S(2)}, u32[]{:S(2)}) collective-permute-start(bf16[384,2304]{1,0:T(8,128)(2,1)S(1)} %fusion.4), channel_id=1, source_target_pairs={{0,1},{1,0},{2,3},{3,2},{4,5},{5,4},{6,7},{7,6},{8,9},{9,8},{10,11... | collective-permute-start | bytes 5308424 | tf_op jit(solution)/shard_map/ppermute | solution.py:23
  71.7 1.7 %bitcast_add_fusion.3 = f32[2,288,1024]{2,1,0:T(8,128)S(1)} fusion(bf16[2,288,1024]{2,1,0:T(8,128)(2,1)} %collective-permute-done.5, f32[2,2,288,1024]{3,2,1,0:T(8,128)S(1)} %bitcast.83, s32[]{:T(128)S(6)} %select_n.126), kind=kLoop, calls=%fused_computation.16 | loop fusion | flops 1179648 | bytes 5898244 | tf_op jit(solution)/shard_map/add | solution.py:115
  74.0 8.5 %collective-permute-done.8 = bf16[288,1024]{1,0:T(8,128)(2,1)S(1)} collective-permute-done((bf16[288,1024]{1,0:T(8,128)(2,1)S(1)}, bf16[288,1024]{1,0:T(8,128)(2,1)S(1)}, u32[]{:S(2)}, u32[]{:S(2)}) %collective-permute-start.8) | collective-permute-done | bytes 589856 | tf_op jit(solution)/shard_map/ppermute | solution.py:33
  82.7 1.9 %collective-permute-start.9 = (bf16[288,1024]{1,0:T(8,128)(2,1)S(1)}, bf16[288,1024]{1,0:T(8,128)(2,1)S(1)}, u32[]{:S(2)}, u32[]{:S(2)}) collective-permute-start(bf16[288,1024]{1,0:T(8,128)(2,1)S(1)} %fusion.32), channel_id=1, source_target_pairs={{0,8},{2,10},{4,12},{6,14},{8,0},{10,2},{12,4},{14,6},{16,24},{18,... | collective-permute-start | bytes 1769480 | tf_op jit(solution)/shard_map/ppermute | solution.py:40
  84.6 1.8 %bitcast_add_fusion = f32[2,288,1024]{2,1,0:T(8,128)S(1)} fusion(bf16[2,288,1024]{2,1,0:T(8,128)(2,1)} %collective-permute-done.13, f32[2,2,288,1024]{3,2,1,0:T(8,128)S(1)} %bitcast.81, s32[]{:T(128)S(6)} %select_n.126), kind=kLoop, calls=%fused_computation.13 | loop fusion | flops 1179648 | bytes 5898244 | tf_op jit(solution)/shard_map/add | solution.py:115
  86.5 1.6 %collective-permute-start.14 = (bf16[288,1024]{1,0:T(8,128)(2,1)S(1)}, bf16[288,1024]{1,0:T(8,128)(2,1)S(1)}, u32[]{:S(2)}, u32[]{:S(2)}) collective-permute-start(bf16[288,1024]{1,0:T(8,128)(2,1)S(1)} %fusion.46), channel_id=1, source_target_pairs={{0,4},{2,6},{4,0},{6,2},{8,12},{10,14},{12,8},{14,10},{16,20},{18,... | collective-permute-start | bytes 1769480 | tf_op jit(solution)/shard_map/ppermute | solution.py:33
  88.0 1.8 %bitcast_add_fusion.1 = f32[2,288,1024]{2,1,0:T(8,128)S(1)} fusion(bf16[2,288,1024]{2,1,0:T(8,128)(2,1)} %collective-permute-done.11, f32[2,2,288,1024]{3,2,1,0:T(8,128)S(1)} %bitcast.79, s32[]{:T(128)S(6)} %select_n.126), kind=kLoop, calls=%fused_computation.14 | loop fusion | flops 1179648 | bytes 5898244 | tf_op jit(solution)/shard_map/add | solution.py:115
  90.5 4.6 %collective-permute-done.6 = bf16[288,1024]{1,0:T(8,128)(2,1)S(1)} collective-permute-done((bf16[288,1024]{1,0:T(8,128)(2,1)S(1)}, bf16[288,1024]{1,0:T(8,128)(2,1)S(1)}, u32[]{:S(2)}, u32[]{:S(2)}) %collective-permute-start.6) | collective-permute-done | bytes 589856 | tf_op jit(solution)/shard_map/ppermute | solution.py:33
  96.6 3.8 %collective-permute-start.16 = (bf16[288,1024]{1,0:T(8,128)(2,1)S(1)}, bf16[288,1024]{1,0:T(8,128)(2,1)S(1)}, u32[]{:S(2)}, u32[]{:S(2)}) collective-permute-start(bf16[288,1024]{1,0:T(8,128)(2,1)S(1)} %fusion.34), channel_id=1, source_target_pairs={{0,24},{2,26},{4,28},{6,30},{8,16},{10,18},{12,20},{14,22},{16,8},... | collective-permute-start | bytes 1769480 | tf_op jit(solution)/shard_map/ppermute | solution.py:40
  100.4 10.0 %collective-permute-done.4 = bf16[384,2304]{1,0:T(8,128)(2,1)S(1)} collective-permute-done((bf16[384,2304]{1,0:T(8,128)(2,1)S(1)}, bf16[384,2304]{1,0:T(8,128)(2,1)S(1)}, u32[]{:S(2)}, u32[]{:S(2)}) %collective-permute-start.4) | collective-permute-done | bytes 1769504 | tf_op jit(solution)/shard_map/ppermute | solution.py:23
  110.4 1.5 %collective-permute-start.10 = (f32[384]{0:T(512)S(1)}, f32[384]{0:T(512)S(1)}, u32[]{:S(2)}, u32[]{:S(2)}) collective-permute-start(f32[384]{0:T(512)S(1)} %get-tuple-element.24), channel_id=1, source_target_pairs={{0,1},{1,0},{2,3},{3,2},{4,5},{5,4},{6,7},{7,6},{8,9},{9,8},{10,11... | collective-permute-start | bytes 4616 | tf_op jit(solution)/shard_map/ppermute | solution.py:23
  111.9 2.5 %multiply_reduce_fusion = (f32[2304]{0:T(1024)S(1)}, f32[384,2304]{1,0:T(8,128)S(1)}) fusion(bf16[384,2304]{1,0:T(8,128)(2,1)S(1)} %copy-done, bf16[384,2304]{1,0:T(8,128)(2,1)S(1)} %collective-permute-done.4, f32[384]{0:T(512)S(1)} %pad_maximum_fusion.3, bf16[384,1024]{1,0:T(8,128)(2,1)S(1)} %get-tuple-element.33, bf16[4608,1024]{1,0:T(8,128)(2,1)S(1)} %bitcast.77, ...), kind=kOutput, calls=%fused_computation.7 | convolution fusion | flops 1817245440 | bytes 12594180 | tf_op jit(solution)/shard_map/dot_general | solution.py:155
  114.7 1.7 %collective-permute-start.15 = (bf16[288,1024]{1,0:T(8,128)(2,1)S(1)}, bf16[288,1024]{1,0:T(8,128)(2,1)S(1)}, u32[]{:S(2)}, u32[]{:S(2)}) collective-permute-start(bf16[288,1024]{1,0:T(8,128)(2,1)S(1)} %fusion.29), channel_id=1, source_target_pairs={{0,8},{2,10},{4,12},{6,14},{8,0},{10,2},{12,4},{14,6},{16,24},{18,... | collective-permute-start | bytes 1769480 | tf_op jit(solution)/shard_map/ppermute | solution.py:40
  116.4 3.1 %collective-permute-done.12 = bf16[288,1024]{1,0:T(8,128)(2,1)S(1)} collective-permute-done((bf16[288,1024]{1,0:T(8,128)(2,1)S(1)}, bf16[288,1024]{1,0:T(8,128)(2,1)S(1)}, u32[]{:S(2)}, u32[]{:S(2)}) %collective-permute-start.12) | collective-permute-done | bytes 589856 | tf_op jit(solution)/shard_map/ppermute | solution.py:33
  119.5 1.7 %collective-permute-start.18 = (f32[2304]{0:T(1024)S(1)}, f32[2304]{0:T(1024)S(1)}, u32[]{:S(2)}, u32[]{:S(2)}) collective-permute-start(f32[2304]{0:T(1024)S(1)} %add.274), channel_id=1, source_target_pairs={{0,4},{2,6},{4,0},{6,2},{8,12},{10,14},{12,8},{14,10},{16,20},{18,... | collective-permute-start | bytes 27656 | tf_op jit(solution)/shard_map/ppermute | solution.py:33
  121.2 2.0 %collective-permute-done.18 = f32[2304]{0:T(1024)S(1)} collective-permute-done((f32[2304]{0:T(1024)S(1)}, f32[2304]{0:T(1024)S(1)}, u32[]{:S(2)}, u32[]{:S(2)}) %collective-permute-start.18) | collective-permute-done | bytes 9248 | tf_op jit(solution)/shard_map/ppermute | solution.py:33
  123.2 3.8 %collective-permute-start.21 = (f32[2304]{0:T(1024)S(1)}, f32[2304]{0:T(1024)S(1)}, u32[]{:S(2)}, u32[]{:S(2)}) collective-permute-start(f32[2304]{0:T(1024)S(1)} %add.275), channel_id=1, source_target_pairs={{0,24},{2,26},{4,28},{6,30},{8,0},{10,2},{12,4},{14,6},{16,8},{18,... | collective-permute-start | bytes 27656 | tf_op jit(solution)/shard_map/ppermute | solution.py:33
  128.0 2.9 %subtract_multiply_fusion = f32[384,2304]{1,0:T(8,128)} fusion(f32[384,2304]{1,0:T(8,128)S(1)} %get-tuple-element.22, bf16[384,2304]{1,0:T(8,128)(2,1)S(1)} %collective-permute-done.4, bf16[384,2304]{1,0:T(8,128)(2,1)S(1)} %copy-done, f32[384]{0:T(512)S(1)} %add_multiply_fusion, f32[2304]{0:T(1024)S(1)} %get-tuple-element.38, f32[384]{0:T(512)S(1)} %pad_maximum_fusion.3), kind=kLoop, calls=%fused_computation.6 | loop fusion | flops 7077888 | bytes 10629120 | tf_op jit(solution)/shard_map/mul | solution.py:164
  130.9 2.3 %collective-permute-done.19 = f32[2304]{0:T(1024)S(1)} collective-permute-done((f32[2304]{0:T(1024)S(1)}, f32[2304]{0:T(1024)S(1)}, u32[]{:S(2)}, u32[]{:S(2)}) %collective-permute-start.19) | collective-permute-done | bytes 9248 | tf_op jit(solution)/shard_map/ppermute | solution.py:33
  (82 shorter events, 21.3 us)
Async XLA Ops:
  0.6 8.7 %copy-start = (bf16[384,2304]{1,0:T(8,128)(2,1)S(1)}, bf16[384,2304]{1,0:T(8,128)(2,1)}, u32[]{:S(2)}) copy-start(bf16[384,2304]{1,0:T(8,128)(2,1)} %param.4) | copy-start | bytes 5308420
  3.4 17.3 %collective-permute-start = (bf16[128,2304]{1,0:T(8,128)(2,1)}, bf16[128,2304]{1,0:T(8,128)(2,1)S(1)}, u32[]{:S(2)}, u32[]{:S(2)}) collective-permute-start(bf16[128,2304]{1,0:T(8,128)(2,1)} %get-tuple-element.15), channel_id=1, source_target_pairs={{0,1},{1,0},{2,3},{3,2},{4,5},{5,4},{6,7},{7,6},{8,9},{9,8},{10,11... | collective-permute-start | bytes 1769480 | tf_op jit(solution)/shard_map/ppermute | solution.py:23
  6.4 41.0 %collective-permute-start.2 = (bf16[128,2304]{1,0:T(8,128)(2,1)}, bf16[128,2304]{1,0:T(8,128)(2,1)S(1)}, u32[]{:S(2)}, u32[]{:S(2)}) collective-permute-start(bf16[128,2304]{1,0:T(8,128)(2,1)} %get-tuple-element.18), channel_id=1, source_target_pairs={{0,1},{1,0},{2,3},{3,2},{4,5},{5,4},{6,7},{7,6},{8,9},{9,8},{10,11... | collective-permute-start | bytes 1769480 | tf_op jit(solution)/shard_map/ppermute | solution.py:23
  6.4 38.8 %collective-permute-start.1 = (bf16[128,2304]{1,0:T(8,128)(2,1)}, bf16[128,2304]{1,0:T(8,128)(2,1)S(1)}, u32[]{:S(2)}, u32[]{:S(2)}) collective-permute-start(bf16[128,2304]{1,0:T(8,128)(2,1)} %get-tuple-element.16), channel_id=1, source_target_pairs={{0,1},{1,0},{2,3},{3,2},{4,5},{5,4},{6,7},{7,6},{8,9},{9,8},{10,11... | collective-permute-start | bytes 1769480 | tf_op jit(solution)/shard_map/ppermute | solution.py:23
  21.3 24.7 %slice-start = ((s8[9437184]{0:T(1024)(128)(4,1)}), s8[4194304]{0:T(1024)(128)(4,1)S(1)}, s32[]{:S(2)}) async-start(s8[9437184]{0:T(1024)(128)(4,1)} %bitcast.76), calls=%async_computation | async-start | bytes 8388608
  21.5 24.4 %slice-start.1 = ((s8[9437184]{0:T(1024)(128)(4,1)}), s8[4194304]{0:T(1024)(128)(4,1)S(1)}, s32[]{:S(2)}) async-start(s8[9437184]{0:T(1024)(128)(4,1)} %bitcast.76), calls=%async_computation.1 | async-start | bytes 8388608
  21.5 24.4 %slice-start.2 = ((s8[9437184]{0:T(1024)(128)(4,1)}), s8[1048576]{0:T(1024)(128)(4,1)S(1)}, s32[]{:S(2)}) async-start(s8[9437184]{0:T(1024)(128)(4,1)} %bitcast.76), calls=%async_computation.2 | async-start | bytes 2097152
  50.1 4.2 %copy-start.1 = (s32[384]{0:T(512)S(1)}, s32[384]{0:T(512)}, u32[]{:S(2)}) copy-start(s32[384]{0:T(512)} %param.7) | copy-start | bytes 4612
  50.6 3.7 %collective-permute-start.3 = (f32[2,384]{1,0:T(2,128)S(1)}, f32[2,384]{1,0:T(2,128)S(1)}, u32[]{:S(2)}, u32[]{:S(2)}) collective-permute-start(f32[2,384]{1,0:T(2,128)S(1)} %pad_maximum_fusion.2), channel_id=1, source_target_pairs={{0,1},{1,0},{2,3},{3,2},{4,5},{5,4},{6,7},{7,6},{8,9},{9,8},{10,11... | collective-permute-start | bytes 9224 | tf_op jit(solution)/shard_map/ppermute | solution.py:23
  56.5 9.0 %collective-permute-start.7 = (bf16[2,288,1024]{2,1,0:T(8,128)(2,1)S(1)}, bf16[2,288,1024]{2,1,0:T(8,128)(2,1)S(1)}, u32[]{:S(2)}, u32[]{:S(2)}) collective-permute-start(bf16[2,288,1024]{2,1,0:T(8,128)(2,1)S(1)} %fusion.26), channel_id=1, source_target_pairs={{0,2},{2,0},{4,6},{6,4},{8,10},{10,8},{12,14},{14,12},{16,18},{18,... | collective-permute-start | bytes 3538952 | tf_op jit(solution)/shard_map/ppermute | solution.py:33
  59.3 12.4 %collective-permute-start.5 = (bf16[2,288,1024]{2,1,0:T(8,128)(2,1)}, bf16[2,288,1024]{2,1,0:T(8,128)(2,1)}, u32[]{:S(2)}, u32[]{:S(2)}) collective-permute-start(bf16[2,288,1024]{2,1,0:T(8,128)(2,1)} %fusion.25), channel_id=1, source_target_pairs={{0,2},{2,0},{4,6},{6,4},{8,10},{10,8},{12,14},{14,12},{16,18},{18,... | collective-permute-start | bytes 3538952 | tf_op jit(solution)/shard_map/ppermute | solution.py:33
  62.4 22.2 %collective-permute-start.13 = (bf16[2,288,1024]{2,1,0:T(8,128)(2,1)}, bf16[2,288,1024]{2,1,0:T(8,128)(2,1)}, u32[]{:S(2)}, u32[]{:S(2)}) collective-permute-start(bf16[2,288,1024]{2,1,0:T(8,128)(2,1)} %fusion.28), channel_id=1, source_target_pairs={{0,2},{2,0},{4,6},{6,4},{8,10},{10,8},{12,14},{14,12},{16,18},{18,... | collective-permute-start | bytes 3538952 | tf_op jit(solution)/shard_map/ppermute | solution.py:33
  65.1 22.9 %collective-permute-start.11 = (bf16[2,288,1024]{2,1,0:T(8,128)(2,1)}, bf16[2,288,1024]{2,1,0:T(8,128)(2,1)}, u32[]{:S(2)}, u32[]{:S(2)}) collective-permute-start(bf16[2,288,1024]{2,1,0:T(8,128)(2,1)} %fusion.27), channel_id=1, source_target_pairs={{0,2},{2,0},{4,6},{6,4},{8,10},{10,8},{12,14},{14,12},{16,18},{18,... | collective-permute-start | bytes 3538952 | tf_op jit(solution)/shard_map/ppermute | solution.py:33
  66.2 16.3 %collective-permute-start.8 = (bf16[288,1024]{1,0:T(8,128)(2,1)S(1)}, bf16[288,1024]{1,0:T(8,128)(2,1)S(1)}, u32[]{:S(2)}, u32[]{:S(2)}) collective-permute-start(bf16[288,1024]{1,0:T(8,128)(2,1)S(1)} %fusion.44), channel_id=1, source_target_pairs={{0,4},{2,6},{4,0},{6,2},{8,12},{10,14},{12,8},{14,10},{16,20},{18,... | collective-permute-start | bytes 1769480 | tf_op jit(solution)/shard_map/ppermute | solution.py:33
  70.1 40.3 %collective-permute-start.4 = (bf16[384,2304]{1,0:T(8,128)(2,1)S(1)}, bf16[384,2304]{1,0:T(8,128)(2,1)S(1)}, u32[]{:S(2)}, u32[]{:S(2)}) collective-permute-start(bf16[384,2304]{1,0:T(8,128)(2,1)S(1)} %fusion.4), channel_id=1, source_target_pairs={{0,1},{1,0},{2,3},{3,2},{4,5},{5,4},{6,7},{7,6},{8,9},{9,8},{10,11... | collective-permute-start | bytes 5308424 | tf_op jit(solution)/shard_map/ppermute | solution.py:23
  73.4 21.7 %collective-permute-start.6 = (bf16[288,1024]{1,0:T(8,128)(2,1)S(1)}, bf16[288,1024]{1,0:T(8,128)(2,1)S(1)}, u32[]{:S(2)}, u32[]{:S(2)}) collective-permute-start(bf16[288,1024]{1,0:T(8,128)(2,1)S(1)} %fusion.43), channel_id=1, source_target_pairs={{0,4},{2,6},{4,0},{6,2},{8,12},{10,14},{12,8},{14,10},{16,20},{18,... | collective-permute-start | bytes 1769480 | tf_op jit(solution)/shard_map/ppermute | solution.py:33
  82.7 13.6 %collective-permute-start.9 = (bf16[288,1024]{1,0:T(8,128)(2,1)S(1)}, bf16[288,1024]{1,0:T(8,128)(2,1)S(1)}, u32[]{:S(2)}, u32[]{:S(2)}) collective-permute-start(bf16[288,1024]{1,0:T(8,128)(2,1)S(1)} %fusion.32), channel_id=1, source_target_pairs={{0,8},{2,10},{4,12},{6,14},{8,0},{10,2},{12,4},{14,6},{16,24},{18,... | collective-permute-start | bytes 1769480 | tf_op jit(solution)/shard_map/ppermute | solution.py:40
  86.5 25.4 %collective-permute-start.14 = (bf16[288,1024]{1,0:T(8,128)(2,1)S(1)}, bf16[288,1024]{1,0:T(8,128)(2,1)S(1)}, u32[]{:S(2)}, u32[]{:S(2)}) collective-permute-start(bf16[288,1024]{1,0:T(8,128)(2,1)S(1)} %fusion.46), channel_id=1, source_target_pairs={{0,4},{2,6},{4,0},{6,2},{8,12},{10,14},{12,8},{14,10},{16,20},{18,... | collective-permute-start | bytes 1769480 | tf_op jit(solution)/shard_map/ppermute | solution.py:33
  89.9 29.5 %collective-permute-start.12 = (bf16[288,1024]{1,0:T(8,128)(2,1)S(1)}, bf16[288,1024]{1,0:T(8,128)(2,1)S(1)}, u32[]{:S(2)}, u32[]{:S(2)}) collective-permute-start(bf16[288,1024]{1,0:T(8,128)(2,1)S(1)} %fusion.45), channel_id=1, source_target_pairs={{0,4},{2,6},{4,0},{6,2},{8,12},{10,14},{12,8},{14,10},{16,20},{18,... | collective-permute-start | bytes 1769480 | tf_op jit(solution)/shard_map/ppermute | solution.py:33
  96.6 37.3 %collective-permute-start.16 = (bf16[288,1024]{1,0:T(8,128)(2,1)S(1)}, bf16[288,1024]{1,0:T(8,128)(2,1)S(1)}, u32[]{:S(2)}, u32[]{:S(2)}) collective-permute-start(bf16[288,1024]{1,0:T(8,128)(2,1)S(1)} %fusion.34), channel_id=1, source_target_pairs={{0,24},{2,26},{4,28},{6,30},{8,16},{10,18},{12,20},{14,22},{16,8},... | collective-permute-start | bytes 1769480 | tf_op jit(solution)/shard_map/ppermute | solution.py:40
  110.4 10.8 %collective-permute-start.10 = (f32[384]{0:T(512)S(1)}, f32[384]{0:T(512)S(1)}, u32[]{:S(2)}, u32[]{:S(2)}) collective-permute-start(f32[384]{0:T(512)S(1)} %get-tuple-element.24), channel_id=1, source_target_pairs={{0,1},{1,0},{2,3},{3,2},{4,5},{5,4},{6,7},{7,6},{8,9},{9,8},{10,11... | collective-permute-start | bytes 4616 | tf_op jit(solution)/shard_map/ppermute | solution.py:23
  114.5 5.0 %collective-permute-start.17 = (f32[2304]{0:T(1024)S(1)}, f32[2304]{0:T(1024)S(1)}, u32[]{:S(2)}, u32[]{:S(2)}) collective-permute-start(f32[2304]{0:T(1024)S(1)} %get-tuple-element.39), channel_id=1, source_target_pairs={{0,2},{2,0},{4,6},{6,4},{8,10},{10,8},{12,14},{14,12},{16,18},{18,... | collective-permute-start | bytes 27656 | tf_op jit(solution)/shard_map/ppermute | solution.py:33
  114.7 19.1 %collective-permute-start.15 = (bf16[288,1024]{1,0:T(8,128)(2,1)S(1)}, bf16[288,1024]{1,0:T(8,128)(2,1)S(1)}, u32[]{:S(2)}, u32[]{:S(2)}) collective-permute-start(bf16[288,1024]{1,0:T(8,128)(2,1)S(1)} %fusion.29), channel_id=1, source_target_pairs={{0,8},{2,10},{4,12},{6,14},{8,0},{10,2},{12,4},{14,6},{16,24},{18,... | collective-permute-start | bytes 1769480 | tf_op jit(solution)/shard_map/ppermute | solution.py:40
  119.5 3.7 %collective-permute-start.18 = (f32[2304]{0:T(1024)S(1)}, f32[2304]{0:T(1024)S(1)}, u32[]{:S(2)}, u32[]{:S(2)}) collective-permute-start(f32[2304]{0:T(1024)S(1)} %add.274), channel_id=1, source_target_pairs={{0,4},{2,6},{4,0},{6,2},{8,12},{10,14},{12,8},{14,10},{16,20},{18,... | collective-permute-start | bytes 27656 | tf_op jit(solution)/shard_map/ppermute | solution.py:33
  123.2 7.7 %collective-permute-start.21 = (f32[2304]{0:T(1024)S(1)}, f32[2304]{0:T(1024)S(1)}, u32[]{:S(2)}, u32[]{:S(2)}) collective-permute-start(f32[2304]{0:T(1024)S(1)} %add.275), channel_id=1, source_target_pairs={{0,24},{2,26},{4,28},{6,30},{8,0},{10,2},{12,4},{14,6},{16,8},{18,... | collective-permute-start | bytes 27656 | tf_op jit(solution)/shard_map/ppermute | solution.py:33
  127.0 6.2 %collective-permute-start.19 = (f32[2304]{0:T(1024)S(1)}, f32[2304]{0:T(1024)S(1)}, u32[]{:S(2)}, u32[]{:S(2)}) collective-permute-start(f32[2304]{0:T(1024)S(1)} %add.275), channel_id=1, source_target_pairs={{0,8},{2,10},{4,12},{6,14},{8,16},{10,18},{12,20},{14,22},{16,24},... | collective-permute-start | bytes 27656 | tf_op jit(solution)/shard_map/ppermute | solution.py:33
  127.0 6.2 %collective-permute-start.20 = (f32[2304]{0:T(1024)S(1)}, f32[2304]{0:T(1024)S(1)}, u32[]{:S(2)}, u32[]{:S(2)}) collective-permute-start(f32[2304]{0:T(1024)S(1)} %add.275), channel_id=1, source_target_pairs={{0,16},{2,18},{4,20},{6,22},{8,24},{10,26},{12,28},{14,30},{16,0},... | collective-permute-start | bytes 27656 | tf_op jit(solution)/shard_map/ppermute | solution.py:33

commit v5 on v3

--- a/solution.py
+++ b/solution.py
@@ -128,7 +128,7 @@
             other = after(other, first)
             second = (mine + other.astype(f32) + first_in.astype(f32)).astype(bf16)
             second_in = dp_to(second, lambda i: na - 1 - i)
-            arrived = [after(p, second) for p in arrived]
+            arrived = [after(p, first) for p in arrived]
             mine, other = halves(near)
             other = after(other, second)
             third = (mine + other.astype(f32)).astype(bf16)

time: 134 us -> 134 us (level)
  other arithmetic: 13.1 us -> 9.45 us
  waiting for transfers between devices: 69.1 us -> 72.6 us
    ppermute x13, waiting for transfers between devices: 19 us -> 24.8 us  [dp_shift(): return lax.ppermute(x, 'dp', pairs)]
    add x4, other arithmetic: 5.82 us -> 2.17 us  [halves(): keep = keep + dp_shift(away, 0, 0, 1).astype(f32)]
    ppermute x13, starting transfers between devices: 11.6 us -> 13 us  [dp_shift(): return lax.ppermute(x, 'dp', pairs)]
  transfers between devices with their start and end apart: 23 -> 23, of which waited for: 13 -> 13; matrix products, arithmetic and copies ran while one was open for 19% -> 15% of each run, Pallas kernels for 0% -> 0%
where the time goes in v5:
time: 134 us
  waiting for transfers between devices  72.6 us (54%)
  starting transfers between devices  28.8 us (21%)
  matrix products  19.6 us (15%)
  other arithmetic  9.45 us (7%)
  local copies, waits for them, and re-layouts  2.57 us (2%)
    ppermute x7, waiting for transfers between devices, shift_tensor(): return lax.ppermute(x, 'tensor', [(i, (i + k) % nt) for i in range(nt)])  47.8 us
    ppermute x13, waiting for transfers between devices, dp_shift(): return lax.ppermute(x, 'dp', pairs)  24.8 us
    ppermute x13, starting transfers between devices, dp_shift(): return lax.ppermute(x, 'dp', pairs)  13 us
    ppermute x7, starting transfers between devices, shift_tensor(): return lax.ppermute(x, 'tensor', [(i, (i + k) % nt) for i in range(nt)])  9.31 us
    ppermute x3, starting transfers between devices, dp_to(): return lax.ppermute(x, 'dp', pairs)  6.51 us
    dot_general x1, matrix products, shards(): lax.dot_general(dlogits, w_block(0), (((1,), (1,)), ((), ())), preferred_...  6 us
    dot_general x4, matrix products, halves(): lax.dot_general(cut, head_grad, (((0,), (0,)), ((), ())), preferred_eleme...  5.76 us
    dot_general x3, matrix products, shards(): logit_parts.append(jnp.dot(full, head, preferred_element_type=f32))  4.62 us
  transfers between devices with their start and end apart: 23, of which 13 were waited for; matrix products, arithmetic and copies ran while one was open for 15% of the time, Pallas kernels for 0%

profile of v5, /device:TPU:0, one launch (start us, length us, event | category | flops | bytes accessed | tf_op | source)
XLA Modules:
  0.0 134.0 jit_solution(8309863042497859982)
XLA Ops:
  1.8 3.0 %collective-permute-start.1 = (bf16[128,2304]{1,0:T(8,128)(2,1)S(1)}, bf16[128,2304]{1,0:T(8,128)(2,1)S(1)}, u32[]{:S(2)}, u32[]{:S(2)}) collective-permute-start(bf16[128,2304]{1,0:T(8,128)(2,1)S(1)} %slice.25), channel_id=1, source_target_pairs={{0,1},{1,0},{2,3},{3,2},{4,5},{5,4},{6,7},{7,6},{8,9},{9,8},{10,11... | collective-permute-start | bytes 1769480 | tf_op jit(solution)/shard_map/ppermute | solution.py:23
  4.8 1.9 %multiply_reduce_fusion.1 = f32[384]{0:T(512)S(1)} fusion(bf16[384,2304]{1,0:T(8,128)(2,1)} %param.4), kind=kLoop, calls=%fused_computation.10 | loop fusion | flops 2653824 | bytes 1771008 | tf_op jit(solution)/shard_map/reduce_sum | solution.py:53
  7.0 11.2 %collective-permute-done = f32[384]{0:T(512)S(1)} collective-permute-done((f32[384]{0:T(512)S(1)}, f32[384]{0:T(512)S(1)}, u32[]{:S(2)}, u32[]{:S(2)}) %collective-permute-start) | collective-permute-done | bytes 1568 | tf_op jit(solution)/shard_map/ppermute | solution.py:23
  18.5 1.8 %collective-permute-start.3 = (bf16[128,2304]{1,0:T(8,128)(2,1)S(1)}, bf16[128,2304]{1,0:T(8,128)(2,1)S(1)}, u32[]{:S(2)}, u32[]{:S(2)}) collective-permute-start(bf16[128,2304]{1,0:T(8,128)(2,1)S(1)} %get-tuple-element.13), channel_id=1, source_target_pairs={{0,1},{1,0},{2,3},{3,2},{4,5},{5,4},{6,7},{7,6},{8,9},{9,8},{10,11... | collective-permute-start | bytes 1769480 | tf_op jit(solution)/shard_map/ppermute | solution.py:23
  21.2 13.6 %collective-permute-done.3 = bf16[128,2304]{1,0:T(8,128)(2,1)S(1)} collective-permute-done((bf16[128,2304]{1,0:T(8,128)(2,1)S(1)}, bf16[128,2304]{1,0:T(8,128)(2,1)S(1)}, u32[]{:S(2)}, u32[]{:S(2)}) %collective-permute-start.3) | collective-permute-done | bytes 589856 | tf_op jit(solution)/shard_map/ppermute | solution.py:23
  34.9 10.9 %collective-permute-done.2 = bf16[128,2304]{1,0:T(8,128)(2,1)S(1)} collective-permute-done((bf16[128,2304]{1,0:T(8,128)(2,1)S(1)}, bf16[128,2304]{1,0:T(8,128)(2,1)S(1)}, u32[]{:S(2)}, u32[]{:S(2)}) %collective-permute-start.2) | collective-permute-done | bytes 589856 | tf_op jit(solution)/shard_map/ppermute | solution.py:23
  46.2 1.5 %fusion.48 = f32[128,1024]{1,0:T(8,128)S(1)} fusion(bf16[128,4608]{1,0:T(8,128)(2,1)S(1)} %get-tuple-element.31, bf16[4608,1024]{1,0:T(8,128)(2,1)S(1)} %copy-done), kind=kOutput, calls=%fused_computation.87 | convolution fusion | flops 1207959552 | bytes 11141120 | tf_op jit(solution)/shard_map/dot_general | solution.py:79
  47.8 1.5 %fusion.47 = f32[128,1024]{1,0:T(8,128)S(1)} fusion(bf16[128,4608]{1,0:T(8,128)(2,1)S(1)} %get-tuple-element.32, bf16[4608,1024]{1,0:T(8,128)(2,1)S(1)} %copy-done), kind=kOutput, calls=%fused_computation.86 | convolution fusion | flops 1207959552 | bytes 11141120 | tf_op jit(solution)/shard_map/dot_general | solution.py:79
  49.3 1.5 %fusion.46 = f32[128,1024]{1,0:T(8,128)S(1)} fusion(bf16[128,4608]{1,0:T(8,128)(2,1)S(1)} %get-tuple-element.30, bf16[4608,1024]{1,0:T(8,128)(2,1)S(1)} %copy-done), kind=kOutput, calls=%fused_computation.85 | convolution fusion | flops 1207959552 | bytes 11141120 | tf_op jit(solution)/shard_map/dot_general | solution.py:79
  51.5 1.5 %collective-permute-start.4 = (f32[2,384]{1,0:T(2,128)S(1)}, f32[2,384]{1,0:T(2,128)S(1)}, u32[]{:S(2)}, u32[]{:S(2)}) collective-permute-start(f32[2,384]{1,0:T(2,128)S(1)} %pad_maximum_fusion.2), channel_id=1, source_target_pairs={{0,1},{1,0},{2,3},{3,2},{4,5},{5,4},{6,7},{7,6},{8,9},{9,8},{10,11... | collective-permute-start | bytes 9224 | tf_op jit(solution)/shard_map/ppermute | solution.py:23
  53.4 1.7 %collective-permute-done.4 = f32[2,384]{1,0:T(2,128)S(1)} collective-permute-done((f32[2,384]{1,0:T(2,128)S(1)}, f32[2,384]{1,0:T(2,128)S(1)}, u32[]{:S(2)}, u32[]{:S(2)}) %collective-permute-start.4) | collective-permute-done | bytes 3104 | tf_op jit(solution)/shard_map/ppermute | solution.py:23
  55.8 3.3 %fusion.4 = bf16[384,2304]{1,0:T(8,128)(2,1)} fusion(bf16[384,1024]{1,0:T(8,128)(2,1)S(1)} %get-tuple-element.22, bf16[4608,1024]{1,0:T(8,128)(2,1)S(1)} %copy-done, s32[]{:T(128)S(6)} %select_n.122), kind=kOutput, calls=%fused_computation.4 | convolution fusion | flops 1812824064 | bytes 7274500 | tf_op jit(solution)/shard_map/dot_general | solution.py:99
  59.1 1.4 %collective-permute-start.5 = (bf16[384,2304]{1,0:T(8,128)(2,1)}, bf16[384,2304]{1,0:T(8,128)(2,1)}, u32[]{:S(2)}, u32[]{:S(2)}) collective-permute-start(bf16[384,2304]{1,0:T(8,128)(2,1)} %fusion.4), channel_id=1, source_target_pairs={{0,1},{1,0},{2,3},{3,2},{4,5},{5,4},{6,7},{7,6},{8,9},{9,8},{10,11... | collective-permute-start | bytes 5308424 | tf_op jit(solution)/shard_map/ppermute | solution.py:23
  60.5 1.4 %fusion.23 = f32[1152,1024]{1,0:T(8,128)S(1)} fusion(bf16[384,1024]{1,0:T(8,128)(2,1)S(1)} %get-tuple-element.22, bf16[384,4608]{1,0:T(8,128)(2,1)S(1)} %pad_maximum_fusion, s32[]{:T(128)S(6)} %select_n.125), kind=kOutput, calls=%fused_computation.53 | convolution fusion | flops 905969664 | bytes 6389764 | tf_op jit(solution)/shard_map/dot_general | solution.py:109
  62.2 1.5 %fusion.17 = f32[1152,1024]{1,0:T(8,128)S(1)} fusion(bf16[384,1024]{1,0:T(8,128)(2,1)S(1)} %get-tuple-element.22, bf16[384,4608]{1,0:T(8,128)(2,1)S(1)} %pad_maximum_fusion, s32[]{:T(128)S(6)} %select_n.135), kind=kOutput, calls=%fused_computation.47 | convolution fusion | flops 905969664 | bytes 6389764 | tf_op jit(solution)/shard_map/dot_general | solution.py:109
  64.4 1.4 %fusion.19 = f32[1152,1024]{1,0:T(8,128)S(1)} fusion(bf16[384,1024]{1,0:T(8,128)(2,1)S(1)} %get-tuple-element.22, bf16[384,4608]{1,0:T(8,128)(2,1)S(1)} %pad_maximum_fusion, s32[]{:T(128)S(6)} %select_n.134), kind=kOutput, calls=%fused_computation.49 | convolution fusion | flops 905969664 | bytes 6389764 | tf_op jit(solution)/shard_map/dot_general | solution.py:109
  66.1 1.4 %fusion.21 = f32[1152,1024]{1,0:T(8,128)S(1)} fusion(bf16[384,1024]{1,0:T(8,128)(2,1)S(1)} %get-tuple-element.22, bf16[384,4608]{1,0:T(8,128)(2,1)S(1)} %pad_maximum_fusion, s32[]{:T(128)S(6)} %select_n.133), kind=kOutput, calls=%fused_computation.51 | convolution fusion | flops 905969664 | bytes 6389764 | tf_op jit(solution)/shard_map/dot_general | solution.py:109
  69.0 1.6 %collective-permute-start.7 = (bf16[288,1024]{1,0:T(8,128)(2,1)S(1)}, bf16[288,1024]{1,0:T(8,128)(2,1)S(1)}, u32[]{:S(2)}, u32[]{:S(2)}) collective-permute-start(bf16[288,1024]{1,0:T(8,128)(2,1)S(1)} %fusion.31), channel_id=1, source_target_pairs={{0,4},{2,6},{4,0},{6,2},{8,12},{10,14},{12,8},{14,10},{16,20},{18,... | collective-permute-start | bytes 1769480 | tf_op jit(solution)/shard_map/ppermute | solution.py:33
  72.4 1.6 %collective-permute-start.12 = (bf16[288,1024]{1,0:T(8,128)(2,1)S(1)}, bf16[288,1024]{1,0:T(8,128)(2,1)S(1)}, u32[]{:S(2)}, u32[]{:S(2)}) collective-permute-start(bf16[288,1024]{1,0:T(8,128)(2,1)S(1)} %fusion.33), channel_id=1, source_target_pairs={{0,4},{2,6},{4,0},{6,2},{8,12},{10,14},{12,8},{14,10},{16,20},{18,... | collective-permute-start | bytes 1769480 | tf_op jit(solution)/shard_map/ppermute | solution.py:33
  74.0 11.2 %collective-permute-done.7 = bf16[288,1024]{1,0:T(8,128)(2,1)S(1)} collective-permute-done((bf16[288,1024]{1,0:T(8,128)(2,1)S(1)}, bf16[288,1024]{1,0:T(8,128)(2,1)S(1)}, u32[]{:S(2)}, u32[]{:S(2)}) %collective-permute-start.7) | collective-permute-done | bytes 589856 | tf_op jit(solution)/shard_map/ppermute | solution.py:33
  85.4 1.6 %collective-permute-start.15 = (bf16[288,1024]{1,0:T(8,128)(2,1)S(1)}, bf16[288,1024]{1,0:T(8,128)(2,1)S(1)}, u32[]{:S(2)}, u32[]{:S(2)}) collective-permute-start(bf16[288,1024]{1,0:T(8,128)(2,1)S(1)} %fusion.16), channel_id=1, source_target_pairs={{0,8},{2,10},{4,12},{6,14},{8,0},{10,2},{12,4},{14,6},{16,24},{18,... | collective-permute-start | bytes 1769480 | tf_op jit(solution)/shard_map/ppermute | solution.py:40
  87.6 9.6 %collective-permute-done.5 = bf16[384,2304]{1,0:T(8,128)(2,1)} collective-permute-done((bf16[384,2304]{1,0:T(8,128)(2,1)}, bf16[384,2304]{1,0:T(8,128)(2,1)}, u32[]{:S(2)}, u32[]{:S(2)}) %collective-permute-start.5) | collective-permute-done | bytes 1769504 | tf_op jit(solution)/shard_map/ppermute | solution.py:23
  98.3 1.6 %collective-permute-start.10 = (bf16[288,1024]{1,0:T(8,128)(2,1)S(1)}, bf16[288,1024]{1,0:T(8,128)(2,1)S(1)}, u32[]{:S(2)}, u32[]{:S(2)}) collective-permute-start(bf16[288,1024]{1,0:T(8,128)(2,1)S(1)} %fusion.32), channel_id=1, source_target_pairs={{0,4},{2,6},{4,0},{6,2},{8,12},{10,14},{12,8},{14,10},{16,20},{18,... | collective-permute-start | bytes 1769480 | tf_op jit(solution)/shard_map/ppermute | solution.py:33
  101.0 3.2 %collective-permute-start.17 = (bf16[288,1024]{1,0:T(8,128)(2,1)S(1)}, bf16[288,1024]{1,0:T(8,128)(2,1)S(1)}, u32[]{:S(2)}, u32[]{:S(2)}) collective-permute-start(bf16[288,1024]{1,0:T(8,128)(2,1)S(1)} %fusion.12), channel_id=1, source_target_pairs={{0,24},{2,26},{4,28},{6,30},{8,16},{10,18},{12,20},{14,22},{16,8},... | collective-permute-start | bytes 1769480 | tf_op jit(solution)/shard_map/ppermute | solution.py:40
  104.3 6.2 %collective-permute-done.12 = bf16[288,1024]{1,0:T(8,128)(2,1)S(1)} collective-permute-done((bf16[288,1024]{1,0:T(8,128)(2,1)S(1)}, bf16[288,1024]{1,0:T(8,128)(2,1)S(1)}, u32[]{:S(2)}, u32[]{:S(2)}) %collective-permute-start.12) | collective-permute-done | bytes 589856 | tf_op jit(solution)/shard_map/ppermute | solution.py:33
  110.7 1.6 %collective-permute-start.16 = (bf16[288,1024]{1,0:T(8,128)(2,1)S(1)}, bf16[288,1024]{1,0:T(8,128)(2,1)S(1)}, u32[]{:S(2)}, u32[]{:S(2)}) collective-permute-start(bf16[288,1024]{1,0:T(8,128)(2,1)S(1)} %fusion.13), channel_id=1, source_target_pairs={{0,8},{2,10},{4,12},{6,14},{8,0},{10,2},{12,4},{14,6},{16,24},{18,... | collective-permute-start | bytes 1769480 | tf_op jit(solution)/shard_map/ppermute | solution.py:40
  112.3 6.0 %multiply_reduce_fusion = (f32[2304]{0:T(1024)S(1)}, f32[384,2304]{1,0:T(8,128)}) fusion(bf16[384,2304]{1,0:T(8,128)(2,1)S(1)} %copy-done.1, bf16[384,2304]{1,0:T(8,128)(2,1)} %collective-permute-done.5, f32[384]{0:T(512)S(1)} %add_rsqrt_fusion, f32[384]{0:T(512)S(1)} %add_multiply_fusion, f32[2304]{0:T(1024)S(1)} %get-tuple-element.29, ...), kind=kOutput, calls=%fused_computation.6 | convolution fusion | flops 1820784384 | bytes 12608516 | tf_op jit(solution)/shard_map/dot_general | solution.py:154
  119.5 1.5 %collective-permute-start.19 = (f32[2304]{0:T(1024)S(1)}, f32[2304]{0:T(1024)S(1)}, u32[]{:S(2)}, u32[]{:S(2)}) collective-permute-start(f32[2304]{0:T(1024)S(1)} %add.234), channel_id=1, source_target_pairs={{0,4},{2,6},{4,0},{6,2},{8,12},{10,14},{12,8},{14,10},{16,20},{18,... | collective-permute-start | bytes 27656 | tf_op jit(solution)/shard_map/ppermute | solution.py:33
  121.0 2.2 %collective-permute-done.19 = f32[2304]{0:T(1024)S(1)} collective-permute-done((f32[2304]{0:T(1024)S(1)}, f32[2304]{0:T(1024)S(1)}, u32[]{:S(2)}, u32[]{:S(2)}) %collective-permute-start.19) | collective-permute-done | bytes 9248 | tf_op jit(solution)/shard_map/ppermute | solution.py:33
  123.2 2.9 %collective-permute-start.22 = (f32[2304]{0:T(1024)S(1)}, f32[2304]{0:T(1024)S(1)}, u32[]{:S(2)}, u32[]{:S(2)}) collective-permute-start(f32[2304]{0:T(1024)S(1)} %add.235), channel_id=1, source_target_pairs={{0,24},{2,26},{4,28},{6,30},{8,0},{10,2},{12,4},{14,6},{16,8},{18,... | collective-permute-start | bytes 27656 | tf_op jit(solution)/shard_map/ppermute | solution.py:33
  127.5 2.0 %collective-permute-start.21 = (f32[2304]{0:T(1024)S(1)}, f32[2304]{0:T(1024)S(1)}, u32[]{:S(2)}, u32[]{:S(2)}) collective-permute-start(f32[2304]{0:T(1024)S(1)} %add.235), channel_id=1, source_target_pairs={{0,16},{2,18},{4,20},{6,22},{8,24},{10,26},{12,28},{14,30},{16,0},... | collective-permute-start | bytes 27656 | tf_op jit(solution)/shard_map/ppermute | solution.py:33
  129.5 2.1 %collective-permute-done.20 = f32[2304]{0:T(1024)S(1)} collective-permute-done((f32[2304]{0:T(1024)S(1)}, f32[2304]{0:T(1024)S(1)}, u32[]{:S(2)}, u32[]{:S(2)}) %collective-permute-start.20) | collective-permute-done | bytes 9248 | tf_op jit(solution)/shard_map/ppermute | solution.py:33
  (73 shorter events, 17.5 us)
Async XLA Ops:
  0.6 6.3 %copy-start.2 = (f32[4608]{0:T(1024)S(1)}, f32[4608]{0:T(1024)}, u32[]{:S(2)}) copy-start(f32[4608]{0:T(1024)} %param.5) | copy-start | bytes 55300
  1.8 16.5 %copy-start.1 = (bf16[384,2304]{1,0:T(8,128)(2,1)S(1)}, bf16[384,2304]{1,0:T(8,128)(2,1)}, u32[]{:S(2)}) copy-start(bf16[384,2304]{1,0:T(8,128)(2,1)} %param.4) | copy-start | bytes 5308420
  1.8 19.4 %collective-permute-start.1 = (bf16[128,2304]{1,0:T(8,128)(2,1)S(1)}, bf16[128,2304]{1,0:T(8,128)(2,1)S(1)}, u32[]{:S(2)}, u32[]{:S(2)}) collective-permute-start(bf16[128,2304]{1,0:T(8,128)(2,1)S(1)} %slice.25), channel_id=1, source_target_pairs={{0,1},{1,0},{2,3},{3,2},{4,5},{5,4},{6,7},{7,6},{8,9},{9,8},{10,11... | collective-permute-start | bytes 1769480 | tf_op jit(solution)/shard_map/ppermute | solution.py:23
  6.7 11.5 %collective-permute-start = (f32[384]{0:T(512)S(1)}, f32[384]{0:T(512)S(1)}, u32[]{:S(2)}, u32[]{:S(2)}) collective-permute-start(f32[384]{0:T(512)S(1)} %multiply_reduce_fusion.1), channel_id=1, source_target_pairs={{0,1},{1,0},{2,3},{3,2},{4,5},{5,4},{6,7},{7,6},{8,9},{9,8},{10,11... | collective-permute-start | bytes 4616 | tf_op jit(solution)/shard_map/ppermute | solution.py:23
  18.3 27.9 %copy-start = (bf16[4608,1024]{1,0:T(8,128)(2,1)S(1)}, bf16[4608,1024]{1,0:T(8,128)(2,1)}, u32[]{:S(2)}) copy-start(bf16[4608,1024]{1,0:T(8,128)(2,1)} %param.6) | copy-start | bytes 28311556
  18.5 16.3 %collective-permute-start.3 = (bf16[128,2304]{1,0:T(8,128)(2,1)S(1)}, bf16[128,2304]{1,0:T(8,128)(2,1)S(1)}, u32[]{:S(2)}, u32[]{:S(2)}) collective-permute-start(bf16[128,2304]{1,0:T(8,128)(2,1)S(1)} %get-tuple-element.13), channel_id=1, source_target_pairs={{0,1},{1,0},{2,3},{3,2},{4,5},{5,4},{6,7},{7,6},{8,9},{9,8},{10,11... | collective-permute-start | bytes 1769480 | tf_op jit(solution)/shard_map/ppermute | solution.py:23
  20.3 25.4 %collective-permute-start.2 = (bf16[128,2304]{1,0:T(8,128)(2,1)S(1)}, bf16[128,2304]{1,0:T(8,128)(2,1)S(1)}, u32[]{:S(2)}, u32[]{:S(2)}) collective-permute-start(bf16[128,2304]{1,0:T(8,128)(2,1)S(1)} %get-tuple-element.12), channel_id=1, source_target_pairs={{0,1},{1,0},{2,3},{3,2},{4,5},{5,4},{6,7},{7,6},{8,9},{9,8},{10,11... | collective-permute-start | bytes 1769480 | tf_op jit(solution)/shard_map/ppermute | solution.py:23
  51.5 3.7 %copy-start.3 = (s32[384]{0:T(512)S(1)}, s32[384]{0:T(512)}, u32[]{:S(2)}) copy-start(s32[384]{0:T(512)} %param.7) | copy-start | bytes 4612
  51.5 3.7 %collective-permute-start.4 = (f32[2,384]{1,0:T(2,128)S(1)}, f32[2,384]{1,0:T(2,128)S(1)}, u32[]{:S(2)}, u32[]{:S(2)}) collective-permute-start(f32[2,384]{1,0:T(2,128)S(1)} %pad_maximum_fusion.2), channel_id=1, source_target_pairs={{0,1},{1,0},{2,3},{3,2},{4,5},{5,4},{6,7},{7,6},{8,9},{9,8},{10,11... | collective-permute-start | bytes 9224 | tf_op jit(solution)/shard_map/ppermute | solution.py:23
  59.1 38.1 %collective-permute-start.5 = (bf16[384,2304]{1,0:T(8,128)(2,1)}, bf16[384,2304]{1,0:T(8,128)(2,1)}, u32[]{:S(2)}, u32[]{:S(2)}) collective-permute-start(bf16[384,2304]{1,0:T(8,128)(2,1)} %fusion.4), channel_id=1, source_target_pairs={{0,1},{1,0},{2,3},{3,2},{4,5},{5,4},{6,7},{7,6},{8,9},{9,8},{10,11... | collective-permute-start | bytes 5308424 | tf_op jit(solution)/shard_map/ppermute | solution.py:23
  62.1 6.2 %collective-permute-start.6 = (bf16[2,288,1024]{2,1,0:T(8,128)(2,1)S(1)}, bf16[2,288,1024]{2,1,0:T(8,128)(2,1)S(1)}, u32[]{:S(2)}, u32[]{:S(2)}) collective-permute-start(bf16[2,288,1024]{2,1,0:T(8,128)(2,1)S(1)} %fusion.7), channel_id=1, source_target_pairs={{0,2},{2,0},{4,6},{6,4},{8,10},{10,8},{12,14},{14,12},{16,18},{18,... | collective-permute-start | bytes 3538952 | tf_op jit(solution)/shard_map/ppermute | solution.py:33
  63.9 6.7 %collective-permute-start.13 = (bf16[2,288,1024]{2,1,0:T(8,128)(2,1)S(1)}, bf16[2,288,1024]{2,1,0:T(8,128)(2,1)S(1)}, u32[]{:S(2)}, u32[]{:S(2)}) collective-permute-start(bf16[2,288,1024]{2,1,0:T(8,128)(2,1)S(1)} %fusion.10), channel_id=1, source_target_pairs={{0,2},{2,0},{4,6},{6,4},{8,10},{10,8},{12,14},{14,12},{16,18},{18,... | collective-permute-start | bytes 3538952 | tf_op jit(solution)/shard_map/ppermute | solution.py:33
  66.0 5.7 %collective-permute-start.11 = (bf16[2,288,1024]{2,1,0:T(8,128)(2,1)S(1)}, bf16[2,288,1024]{2,1,0:T(8,128)(2,1)S(1)}, u32[]{:S(2)}, u32[]{:S(2)}) collective-permute-start(bf16[2,288,1024]{2,1,0:T(8,128)(2,1)S(1)} %fusion.9), channel_id=1, source_target_pairs={{0,2},{2,0},{4,6},{6,4},{8,10},{10,8},{12,14},{14,12},{16,18},{18,... | collective-permute-start | bytes 3538952 | tf_op jit(solution)/shard_map/ppermute | solution.py:33
  67.7 19.3 %collective-permute-start.9 = (bf16[2,288,1024]{2,1,0:T(8,128)(2,1)S(1)}, bf16[2,288,1024]{2,1,0:T(8,128)(2,1)S(1)}, u32[]{:S(2)}, u32[]{:S(2)}) collective-permute-start(bf16[2,288,1024]{2,1,0:T(8,128)(2,1)S(1)} %fusion.8), channel_id=1, source_target_pairs={{0,2},{2,0},{4,6},{6,4},{8,10},{10,8},{12,14},{14,12},{16,18},{18,... | collective-permute-start | bytes 3538952 | tf_op jit(solution)/shard_map/ppermute | solution.py:33
  69.0 16.3 %collective-permute-start.7 = (bf16[288,1024]{1,0:T(8,128)(2,1)S(1)}, bf16[288,1024]{1,0:T(8,128)(2,1)S(1)}, u32[]{:S(2)}, u32[]{:S(2)}) collective-permute-start(bf16[288,1024]{1,0:T(8,128)(2,1)S(1)} %fusion.31), channel_id=1, source_target_pairs={{0,4},{2,6},{4,0},{6,2},{8,12},{10,14},{12,8},{14,10},{16,20},{18,... | collective-permute-start | bytes 1769480 | tf_op jit(solution)/shard_map/ppermute | solution.py:33
  71.2 28.7 %collective-permute-start.14 = (bf16[288,1024]{1,0:T(8,128)(2,1)S(1)}, bf16[288,1024]{1,0:T(8,128)(2,1)S(1)}, u32[]{:S(2)}, u32[]{:S(2)}) collective-permute-start(bf16[288,1024]{1,0:T(8,128)(2,1)S(1)} %fusion.34), channel_id=1, source_target_pairs={{0,4},{2,6},{4,0},{6,2},{8,12},{10,14},{12,8},{14,10},{16,20},{18,... | collective-permute-start | bytes 1769480 | tf_op jit(solution)/shard_map/ppermute | solution.py:33
  72.4 38.1 %collective-permute-start.12 = (bf16[288,1024]{1,0:T(8,128)(2,1)S(1)}, bf16[288,1024]{1,0:T(8,128)(2,1)S(1)}, u32[]{:S(2)}, u32[]{:S(2)}) collective-permute-start(bf16[288,1024]{1,0:T(8,128)(2,1)S(1)} %fusion.33), channel_id=1, source_target_pairs={{0,4},{2,6},{4,0},{6,2},{8,12},{10,14},{12,8},{14,10},{16,20},{18,... | collective-permute-start | bytes 1769480 | tf_op jit(solution)/shard_map/ppermute | solution.py:33
  85.4 15.3 %collective-permute-start.15 = (bf16[288,1024]{1,0:T(8,128)(2,1)S(1)}, bf16[288,1024]{1,0:T(8,128)(2,1)S(1)}, u32[]{:S(2)}, u32[]{:S(2)}) collective-permute-start(bf16[288,1024]{1,0:T(8,128)(2,1)S(1)} %fusion.16), channel_id=1, source_target_pairs={{0,8},{2,10},{4,12},{6,14},{8,0},{10,2},{12,4},{14,6},{16,24},{18,... | collective-permute-start | bytes 1769480 | tf_op jit(solution)/shard_map/ppermute | solution.py:40
  97.2 3.6 %collective-permute-start.8 = (f32[384]{0:T(512)S(1)}, f32[384]{0:T(512)S(1)}, u32[]{:S(2)}, u32[]{:S(2)}) collective-permute-start(f32[384]{0:T(512)S(1)} %get-tuple-element.15), channel_id=1, source_target_pairs={{0,1},{1,0},{2,3},{3,2},{4,5},{5,4},{6,7},{7,6},{8,9},{9,8},{10,11... | collective-permute-start | bytes 4616 | tf_op jit(solution)/shard_map/ppermute | solution.py:23
  98.3 34.3 %collective-permute-start.10 = (bf16[288,1024]{1,0:T(8,128)(2,1)S(1)}, bf16[288,1024]{1,0:T(8,128)(2,1)S(1)}, u32[]{:S(2)}, u32[]{:S(2)}) collective-permute-start(bf16[288,1024]{1,0:T(8,128)(2,1)S(1)} %fusion.32), channel_id=1, source_target_pairs={{0,4},{2,6},{4,0},{6,2},{8,12},{10,14},{12,8},{14,10},{16,20},{18,... | collective-permute-start | bytes 1769480 | tf_op jit(solution)/shard_map/ppermute | solution.py:33
  101.0 31.6 %collective-permute-start.17 = (bf16[288,1024]{1,0:T(8,128)(2,1)S(1)}, bf16[288,1024]{1,0:T(8,128)(2,1)S(1)}, u32[]{:S(2)}, u32[]{:S(2)}) collective-permute-start(bf16[288,1024]{1,0:T(8,128)(2,1)S(1)} %fusion.12), channel_id=1, source_target_pairs={{0,24},{2,26},{4,28},{6,30},{8,16},{10,18},{12,20},{14,22},{16,8},... | collective-permute-start | bytes 1769480 | tf_op jit(solution)/shard_map/ppermute | solution.py:40
  110.7 22.0 %collective-permute-start.16 = (bf16[288,1024]{1,0:T(8,128)(2,1)S(1)}, bf16[288,1024]{1,0:T(8,128)(2,1)S(1)}, u32[]{:S(2)}, u32[]{:S(2)}) collective-permute-start(bf16[288,1024]{1,0:T(8,128)(2,1)S(1)} %fusion.13), channel_id=1, source_target_pairs={{0,8},{2,10},{4,12},{6,14},{8,0},{10,2},{12,4},{14,6},{16,24},{18,... | collective-permute-start | bytes 1769480 | tf_op jit(solution)/shard_map/ppermute | solution.py:40
  118.3 1.2 collective-permute-start.18
  119.5 3.7 %collective-permute-start.19 = (f32[2304]{0:T(1024)S(1)}, f32[2304]{0:T(1024)S(1)}, u32[]{:S(2)}, u32[]{:S(2)}) collective-permute-start(f32[2304]{0:T(1024)S(1)} %add.234), channel_id=1, source_target_pairs={{0,4},{2,6},{4,0},{6,2},{8,12},{10,14},{12,8},{14,10},{16,20},{18,... | collective-permute-start | bytes 27656 | tf_op jit(solution)/shard_map/ppermute | solution.py:33
  123.2 4.3 %collective-permute-start.22 = (f32[2304]{0:T(1024)S(1)}, f32[2304]{0:T(1024)S(1)}, u32[]{:S(2)}, u32[]{:S(2)}) collective-permute-start(f32[2304]{0:T(1024)S(1)} %add.235), channel_id=1, source_target_pairs={{0,24},{2,26},{4,28},{6,30},{8,0},{10,2},{12,4},{14,6},{16,8},{18,... | collective-permute-start | bytes 27656 | tf_op jit(solution)/shard_map/ppermute | solution.py:33
  126.1 5.5 %collective-permute-start.20 = (f32[2304]{0:T(1024)S(1)}, f32[2304]{0:T(1024)S(1)}, u32[]{:S(2)}, u32[]{:S(2)}) collective-permute-start(f32[2304]{0:T(1024)S(1)} %add.235), channel_id=1, source_target_pairs={{0,8},{2,10},{4,12},{6,14},{8,16},{10,18},{12,20},{14,22},{16,24},... | collective-permute-start | bytes 27656 | tf_op jit(solution)/shard_map/ppermute | solution.py:33
  127.5 4.6 %collective-permute-start.21 = (f32[2304]{0:T(1024)S(1)}, f32[2304]{0:T(1024)S(1)}, u32[]{:S(2)}, u32[]{:S(2)}) collective-permute-start(f32[2304]{0:T(1024)S(1)} %add.235), channel_id=1, source_target_pairs={{0,16},{2,18},{4,20},{6,22},{8,24},{10,26},{12,28},{14,30},{16,0},... | collective-permute-start | bytes 27656 | tf_op jit(solution)/shard_map/ppermute | solution.py:33
